TPU v7x, 32 devices: a whole 2x2x4 slice. The times are simulated.
32 devices in a mesh: groups: 2 (over y), segment: 4 (over z), rows: 4 (over x, core).
Axes of the slice: x: 2, y: 2, z: 4, core: 2. Of those that a mesh axis runs over, the one named last changes fastest.
Arguments:
- hidden: bfloat16 [2, 32, 16, 320], P('groups', 'rows'), parts along dimension 0, may hold values from -36 to 36
- timesteps: int32 [2], P('groups'), parts along dimension 0, may hold values from 0 to 999
- rule_matrices: float32 [4, 4, 4, 4], P('segment'), may hold values from -2 to 2
- conv_factors: bfloat16 [4, 9, 4, 80, 80], P('segment'), may hold values from -0.0546875 to 0.0546875
- time_proj: bfloat16 [4, 320, 320], P('segment'), may hold values from -0.15625 to 0.15625
- skip_factors: bfloat16 [4, 4, 80, 80], P('segment'), may hold values from -0.15625 to 0.15625
- attn_factors: bfloat16 [4, 4, 4, 80, 80], P('segment'), may hold values from -0.3125 to 0.3125
- up_factors: bfloat16 [4, 4, 80, 320], P('segment'), may hold values from -0.3125 to 0.3125
- down_factors: bfloat16 [4, 4, 320, 80], P('segment'), may hold values from -0.15625 to 0.15625
- norm_gains: float32 [4, 3, 320], P('segment'), may hold values from 0.25 to 1.75
- head_scales: float32 [4, 5], P('segment'), may hold values from 3 to 12
- has_block: int32 [4], P('segment'), may hold values 0 or 1
- offsets: int32 [4], P('segment'), may hold values from 0 to 7
Outputs:
- states: bfloat16 [4, 2, 32, 16, 320], P('segment', 'groups', 'rows'), parts along dimension 1
There are 2 independent parts, one for each index of `groups`. A program takes and returns all parts, laid end to end along the dimension named above; an argument that names none is the same for every part. Nothing has to cross between parts.
All inputs are finite; a program needn't handle non-finite values. No bound on the sum of `has_block` on one device may be relied on, other than what follows from the above.
Results may differ from a plain program's by a relative error of at most 0.0062.
Values may be sent and summed in bfloat16 or wider, within the bound.
No kernel may reach another device: no remote copies, remote signals or barrier semaphores. Data moves between devices by JAX's collectives and lax.ppermute only.
A program may use at most 64 MiB of HBM per device.

v0:
```python
import functools
import math

import jax
import jax.numpy as jnp
from jax import lax
from jax.experimental import pallas as pl
from jax.experimental.pallas import tpu as pltpu
from jax.sharding import PartitionSpec as P

HEAD = 64
WIN = 8
QUAT = 4

EPSILON = 1e-05
COS_EPSILON = 1e-06

F32 = jnp.float32
BF16 = jnp.bfloat16
MIB = 1024 * 1024
LANES = 128

VMEM = pl.BlockSpec(memory_space=pltpu.VMEM)
SMEM = pl.BlockSpec(memory_space=pltpu.SMEM)
HBM = pl.BlockSpec(memory_space=pltpu.HBM)


def in_vmem(value):
    return pltpu.with_memory_space_constraint(value, pltpu.VMEM)


def in_smem(value):
    return pltpu.with_memory_space_constraint(value, pltpu.SMEM)


def in_hbm(value):
    return pltpu.with_memory_space_constraint(value, pltpu.HBM)


def dot(left, right):
    return jnp.dot(left, right, preferred_element_type=F32)


def dot_t(left, right):
    return lax.dot_general(left, right, (((1,), (1,)), ((), ())), preferred_element_type=F32)


def rms(values, gain_row):
    mean_square = jnp.mean(values * values, axis=-1, keepdims=True)
    return values * lax.rsqrt(mean_square + EPSILON) * gain_row


def silu(values):
    return values / (1.0 + jnp.exp(-values))


def weights_kernel(
    first_skip, rule_hbm, time_hbm, flag_hbm, offset_hbm, scale_hbm, gain_hbm,
    conv_hbm, attn_hbm, up_hbm, down_hbm, skip_hbm, proj_hbm, hidden_hbm,
    mix_out, qkv_out, out_out, up_out, down_out, term_out, gain_out, meta_out, scale_out,
    hidden_out,
    rule_ref, time_ref, flag_ref, offset_ref, conv_ref, attn_ref, up_ref, down_ref,
    skip_ref, proj_ref, rows_ref, sems,
):
    sources = [
        rule_hbm, conv_hbm, skip_hbm, time_hbm, proj_hbm, flag_hbm, offset_hbm, scale_hbm,
        gain_hbm, hidden_hbm, attn_hbm, up_hbm, down_hbm,
    ]
    targets = [
        rule_ref, conv_ref, skip_ref, time_ref, proj_ref, flag_ref, offset_ref, scale_out,
        gain_out, hidden_out, attn_ref, up_ref, down_ref,
    ]
    copies = [
        pltpu.make_async_copy(source, target, sems.at[place])
        for place, (source, target) in enumerate(zip(sources, targets))
    ]
    for copy in copies:
        copy.start()
    part = conv_ref.shape[-1]

    def rule(i, a, b):
        return rule_ref[i, a, b]

    def block_row(factors, a):
        blocks = []
        for b in range(QUAT):
            total = factors[0] * rule(0, a, b)
            for i in range(1, QUAT):
                total = total + factors[i] * rule(i, a, b)
            blocks.append(total)
        return blocks

    channels = proj_ref.shape[0]
    tail = channels % LANES
    full = channels - tail
    padded = full + LANES

    def channel_of(lane):
        return jnp.where(lane < channels, lane, lane - tail)

    lanes = channel_of(lax.broadcasted_iota(jnp.int32, (part, padded), 1))
    ones = lax.rem(lanes, part) == lax.broadcasted_iota(jnp.int32, (part, padded), 0)
    repeat = jnp.where(ones, 1.0, 0.0).astype(BF16)
    copies[0].wait()
    block = channel_of(lax.broadcasted_iota(jnp.int32, (8, padded), 1)) // part
    for i in range(QUAT):
        for a in range(QUAT):
            row = jnp.where(block == 0, rule(i, a, 0), rule(i, a, 1))
            row = jnp.where(block == 2, rule(i, a, 2), row)
            rows_ref[i * QUAT + a] = jnp.where(block == 3, rule(i, a, 3), row)

    def square(factors, store):
        stacked = factors.reshape(QUAT * part, part)
        for tile in range(padded // LANES):
            at = slice(tile * LANES, (tile + 1) * LANES)
            rows = [rows_ref[place, :, at][None] for place in range(QUAT * QUAT)]
            whole = dot(stacked, repeat[:, at])
            for chunk in range(part // 16):
                spread = [
                    whole[i * part + chunk * 16 : i * part + (chunk + 1) * 16]
                    for i in range(QUAT)
                ]
                spread = [value.reshape(2, 8, LANES) for value in spread]
                for a in range(QUAT):
                    total = spread[0] * rows[a]
                    for i in range(1, QUAT):
                        total = total + spread[i] * rows[i * QUAT + a]
                    start = a * part + chunk * 16
                    store(tile, slice(start, start + 16), total.reshape(16, LANES).astype(BF16))

    def store_plain(out):
        def store(tile, rows, value):
            width = min(LANES, channels - tile * LANES)
            out[rows, tile * LANES : tile * LANES + width] = value[:, :width]

        return store

    def store_heads(which):
        def store(tile, rows, value):
            if tile * LANES < full:
                at, low, high = which * full + tile * LANES, 0, LANES
            else:
                at, low = 3 * full + which // 2 * LANES, which % 2 * tail
                high = LANES if which == 2 else low + tail
            qkv_out[rows, at + low : at + high] = value[:, low:high]

        return store

    copies[1].wait()
    for tap in range(9):
        square(conv_ref[tap], store_plain(mix_out.at[tap]))
    copies[2].wait()

    @pl.when(lax.axis_index("segment") >= first_skip)
    def _():
        square(skip_ref[...], store_plain(mix_out.at[9]))

    for copy in copies[3:10]:
        copy.wait()
    half = channels // 2
    lane = lax.broadcasted_iota(jnp.int32, (8, channels), 1)
    place = jnp.where(lane < half, lane, lane - half).astype(F32)
    frequency = jnp.exp(-math.log(10000.0) * place / half)
    for batch in range(term_out.shape[0]):
        angles = time_ref[batch].astype(F32) * frequency
        features = jnp.where(lane < half, jnp.cos(angles), jnp.sin(angles)).astype(BF16)
        term_out[batch] = dot(features, proj_ref[...])
    meta_out[0] = flag_ref[0]
    meta_out[1] = offset_ref[0]
    for copy in copies[10:]:
        copy.wait()

    @pl.when(flag_ref[0] == 1)
    def _():
        for which in range(3):
            square(attn_ref[which], store_heads(which))
        square(attn_ref[3], store_plain(out_out))

        def store_wide(out, place, rows, value):
            out[rows, place * full : (place + 1) * full] = value[:, :full].astype(BF16)
            at, low = QUAT * full + place // 2 * LANES, place % 2 * tail
            half_tile = value[:, full + low : full + low + tail].astype(BF16)
            out[rows, at + low : at + low + tail] = half_tile

        def widen(value):
            value = value.astype(F32)
            return jnp.concatenate([value, value[:, full:]], axis=1)

        def wide_step(chunk, carry):
            start = pl.multiple_of(chunk * 16, 16)
            ups = [widen(up_ref[i, pl.ds(start, 16), :]) for i in range(QUAT)]
            downs = [widen(down_ref[i, pl.ds(start, 16), :]) for i in range(QUAT)]
            for a in range(QUAT):
                rows = pl.ds(pl.multiple_of(a * part + start, 16), 16)
                for b, value in enumerate(block_row(ups, a)):
                    store_wide(up_out, b, rows, value)
            for b in range(QUAT):
                rows = pl.ds(pl.multiple_of(b * part + start, 16), 16)
                for a in range(QUAT):
                    total = downs[0] * rule(0, a, b)
                    for i in range(1, QUAT):
                        total = total + downs[i] * rule(i, a, b)
                    store_wide(down_out, a, rows, total)
            return carry

        lax.fori_loop(0, part // 16, wide_step, 0)


def section_weights(
    first_skip, rule, timesteps, flag, offset, scales, gains, conv, attn, up, down, skip, proj, hidden
):
    channels = proj.shape[0]
    padded = channels // LANES * LANES + LANES
    wide = up.shape[-1]
    operands = (
        rule, timesteps, flag, offset, scales, gains, conv, attn, up, down, skip, proj, hidden,
    )
    return pl.pallas_call(
        functools.partial(weights_kernel, first_skip),
        out_shape=(
            pltpu.VMEM((10, channels, channels), BF16),
            pltpu.VMEM((channels, 8 * LANES), BF16),
            pltpu.VMEM((channels, channels), BF16),
            pltpu.VMEM((channels, QUAT * wide), BF16),
            pltpu.VMEM((channels, QUAT * wide), BF16),
            pltpu.VMEM((hidden.shape[0], 8, channels), F32),
            pltpu.VMEM(gains.shape, F32),
            pltpu.SMEM((2,), jnp.int32),
            pltpu.SMEM(scales.shape, F32),
            pltpu.VMEM(hidden.shape, BF16),
        ),
        in_specs=[HBM] * len(operands),
        out_specs=(VMEM,) * 7 + (SMEM,) * 2 + (VMEM,),
        scratch_shapes=[
            pltpu.SMEM(rule.shape, F32),
            pltpu.SMEM(timesteps.shape, jnp.int32),
            pltpu.SMEM((1,), jnp.int32),
            pltpu.SMEM((1,), jnp.int32),
        ]
        + [pltpu.VMEM(array.shape, BF16) for array in (conv, attn, up, down, skip, proj)]
        + [
            pltpu.VMEM((QUAT * QUAT, 8, padded), F32),
            pltpu.SemaphoreType.DMA((len(operands),)),
        ],
        compiler_params=pltpu.CompilerParams(vmem_limit_bytes=12 * MIB),
        name="weights",
    )(*[in_hbm(v) if v.size > 1 else v for v in operands])


def is_active(tick, batches):
    batch = tick - lax.axis_index("segment")
    return (batch >= 0) & (batch < batches)


def shift_columns(normed, columns):
    total = normed.shape[0]
    col = lax.rem(lax.broadcasted_iota(jnp.int32, (total, 1), 0), columns)
    left = jnp.where(col == 0, 0.0, pltpu.roll(normed, 1, 0)).astype(BF16)
    right = jnp.where(col == columns - 1, 0.0, pltpu.roll(normed, total - 1, 0)).astype(BF16)
    return [left, normed.astype(BF16), right]


def inner_kernel(columns, tick, batches, with_skip, *refs):
    if tick is None:
        tick_ref, *refs = refs
        tick = tick_ref[0]
    if with_skip:
        z_ref, *refs = refs
    x_ref, mix_ref, term_ref, gain_ref, sum_ref = refs
    tokens, channels = x_ref.shape

    @pl.when(is_active(tick, batches))
    def _():
        shifted = shift_columns(rms(x_ref[...].astype(F32), gain_ref[0]), columns)
        edge = jnp.zeros((columns, channels), BF16)
        hidden = jnp.broadcast_to(term_ref[0:1, :], (tokens, channels))
        if with_skip:
            hidden = hidden + dot(z_ref[...], mix_ref[9])
        for b in range(3):
            hidden = hidden + dot(shifted[b], mix_ref[3 + b])
        for b in range(3):
            rows = jnp.concatenate([edge, shifted[b][: tokens - columns]], axis=0)
            hidden = hidden + dot(rows, mix_ref[b])
        for b in range(3):
            rows = jnp.concatenate([shifted[b][columns:], edge], axis=0)
            hidden = hidden + dot(rows, mix_ref[6 + b])
        sum_ref[...] = hidden


def attention(normed, qkv_ref, scales_ref, offset, columns):
    tokens = normed.shape[0]
    projected = dot(normed, qkv_ref[...]).astype(BF16)
    tiles = [projected[:, t * LANES : (t + 1) * LANES] for t in range(8)]
    lane = lax.broadcasted_iota(jnp.int32, (tokens, LANES), 1)
    left = lane < HEAD

    groups = lax.broadcasted_iota(jnp.int32, (LANES, LANES), 0) // HEAD
    groups = groups == lax.broadcasted_iota(jnp.int32, (LANES, LANES), 1) // HEAD
    groups = jnp.where(groups, 1.0, 0.0).astype(BF16)
    scaled = [tiles[t].astype(F32) for t in (0, 1, 2, 3, 6)]
    squares = jnp.concatenate([(v * v).astype(BF16) for v in scaled], axis=0)
    inverse = lax.rsqrt(dot(squares, groups) + COS_EPSILON)
    factors = [
        jnp.where(left, scales_ref[0, 0], scales_ref[0, 1]),
        jnp.where(left, scales_ref[0, 2], scales_ref[0, 3]),
        None,
        None,
        jnp.where(left, scales_ref[0, 4], 1.0),
    ]
    units = []
    for place, (value, factor) in enumerate(zip(scaled, factors)):
        norm = inverse[place * tokens : (place + 1) * tokens]
        units.append(value * (norm if factor is None else norm * factor))
    last_key = pltpu.roll(units[4], HEAD, 1).astype(BF16)
    units = [value.astype(BF16) for value in units]

    def window(index):
        return lax.rem(lax.rem(index, columns) - offset + columns, columns) // WIN

    row_window = window(lax.broadcasted_iota(jnp.int32, (tokens, 1), 0))
    same = row_window == window(lax.broadcasted_iota(jnp.int32, (1, tokens), 1))
    zero, one = jnp.zeros((), BF16), jnp.ones((), BF16)

    def weights(query, keys):
        return jnp.where(same, jnp.exp(dot_t(query, keys)), 0.0).astype(BF16)

    mixed = []
    for t in range(2):
        even = weights(jnp.where(left, units[t], zero), units[2 + t])
        odd = weights(jnp.where(left, zero, units[t]), units[2 + t])
        even = dot(even, jnp.where(left, tiles[4 + t], one))
        odd = dot(odd, jnp.where(left, one, tiles[4 + t]))
        sums = pltpu.roll(jnp.where(left, odd, even), HEAD, 1)
        mixed.append((jnp.where(left, even, odd) / sums).astype(BF16))
    even = weights(jnp.where(left, units[4], zero), last_key)
    even = dot(even, jnp.where(left, tiles[7], one))
    mixed.append((even / pltpu.roll(even, HEAD, 1)).astype(BF16)[:, :HEAD])
    return jnp.concatenate(mixed, axis=1)


def outer_kernel(columns, tick, batches, *refs):
    if tick is None:
        tick_ref, *refs = refs
        tick = tick_ref[0]
    (
        meta_ref, scales_ref, x_ref, sum_ref, low_ref, high_ref, prev_ref, mix_ref, qkv_ref,
        proj_ref, up_ref, down_ref, gain_ref, out_ref, first_ref, last_ref,
    ) = refs
    tokens, channels = x_ref.shape
    active = is_active(tick, batches)

    def write(x3):
        value = x3.astype(BF16)
        out_ref[...] = value
        first_ref[...] = value[:columns]
        last_ref[...] = value[tokens - columns :]

    @pl.when(jnp.logical_not(active))
    def _():
        out_ref[...] = prev_ref[...]

    @pl.when(active)
    def _():
        gain = [gain_ref[row] for row in range(3)]
        below = low_ref.shape[0] - columns
        low = shift_columns(rms(low_ref[below:].astype(F32), gain[0]), columns)
        high = shift_columns(rms(high_ref[:columns].astype(F32), gain[0]), columns)
        top = sum_ref[:columns]
        bottom = sum_ref[tokens - columns :]
        for b in range(3):
            top = top + dot(low[b], mix_ref[b])
            bottom = bottom + dot(high[b], mix_ref[6 + b])
        hidden = jnp.concatenate([top, sum_ref[columns : tokens - columns], bottom], axis=0)
        x1 = x_ref[...].astype(F32) + silu(hidden)
        has_block, offset = meta_ref[0], meta_ref[1]

        @pl.when(has_block != 1)
        def _():
            write(x1)

        @pl.when(has_block == 1)
        def _():
            n2 = rms(x1, gain[1]).astype(BF16)
            heads = attention(n2, qkv_ref, scales_ref, offset, columns)
            x2 = x1 + dot(heads, proj_ref[...])
            n3 = rms(x2, gain[2]).astype(BF16)
            act = silu(dot(n3, up_ref[...])).astype(BF16)
            x3 = x2 + dot_t(act, down_ref[...])
            write(x3)


def run_inner(columns, tick, batches, x, z, mix, term, gains):
    static = isinstance(tick, int)
    with_skip = z is not None
    operands = [z] if with_skip else []
    operands += [x, in_vmem(mix), term, in_vmem(gains)]
    specs = [VMEM] * len(operands)
    if not static:
        operands, specs = [tick] + operands, [SMEM] + specs
    return pl.pallas_call(
        functools.partial(inner_kernel, columns, tick if static else None, batches, with_skip),
        out_shape=pltpu.VMEM(x.shape, F32),
        in_specs=specs,
        out_specs=VMEM,
        compiler_params=pltpu.CompilerParams(vmem_limit_bytes=8 * MIB),
        name="inner",
    )(*operands)


def run_outer(columns, tick, batches, x, total, low, high, prev, weights):
    static = isinstance(tick, int)
    mix, qkv, proj, up, down, gains, meta, scales = weights
    operands = [in_smem(meta), in_smem(scales), x, in_vmem(total), low, high, prev]
    operands += [in_vmem(w) for w in (mix, qkv, proj, up, down, gains)]
    specs = [SMEM] * 2 + [VMEM] * (len(operands) - 2)
    if not static:
        operands, specs = [tick] + operands, [SMEM] + specs
    edge = jax.ShapeDtypeStruct((columns, x.shape[1]), BF16)
    return pl.pallas_call(
        functools.partial(outer_kernel, columns, tick if static else None, batches),
        out_shape=(jax.ShapeDtypeStruct(x.shape, BF16), edge, edge),
        in_specs=specs,
        out_specs=(VMEM,) * 3,
        compiler_params=pltpu.CompilerParams(vmem_limit_bytes=8 * MIB),
        name="outer",
    )(*operands)


def shards(
    hidden, timesteps, rule_matrices, conv_factors, time_proj, skip_factors, attn_factors,
    up_factors, down_factors, norm_gains, head_scales, has_block, offsets,
):
    segments = lax.axis_size("segment")
    row_parts = lax.axis_size("rows")
    half = segments // 2
    segment = lax.axis_index("segment")
    batches, height, columns, channels = hidden.shape
    tokens = height * columns
    axes = ("segment", "rows")

    def pairs(sources, step, turn):
        return [
            (s * row_parts + r, (s + step) * row_parts + r + turn)
            for s in sources
            for r in range(row_parts)
            if 0 <= s + step < segments and 0 <= r + turn < row_parts
        ]

    def pass_on(value, sources, step, turn):
        links = pairs(sources, step, turn)
        if not links:
            return jnp.zeros_like(value)
        return lax.ppermute(value, axes, links)

    flat = hidden.reshape(batches, tokens, channels)
    near, far = min(1, segments - 1), min(2, segments - 1)
    low0 = pass_on(flat, [near], -near, 1)
    high0 = pass_on(flat, [far], -far, -1)
    mix, qkv, proj, up, down, terms, gains, meta, scales, flat = section_weights(
        half if batches == 1 else 0,
        rule_matrices[0], timesteps, has_block, offsets, head_scales,
        jnp.transpose(norm_gains, (1, 0, 2)), conv_factors[0], attn_factors[0], up_factors[0],
        jnp.transpose(down_factors[0], (0, 2, 1)), skip_factors[0], time_proj[0], flat,
    )
    weights = (mix, qkv, proj, up, down, gains, meta, scales)

    def section(tick, x, low, high, z, prev, term):
        total = run_inner(columns, tick, batches, x, z, mix, term, gains)
        return run_outer(columns, tick, batches, x, total, low, high, prev, weights)

    def edges_on(out, first, last, sources):
        main = pass_on(out, sources, 1, 0)
        low = pass_on(last, sources, 1, 1)
        high = pass_on(first, sources, 1, -1)
        return main, low, high

    if batches == 1:
        x, low, high = flat[0], low0[0], high0[0]
        out = flat[0]
        skips = []
        for tick in range(segments):
            z = skips[tick - half] if tick >= half else None
            out, first, last = section(tick, x, low, high, z, out, terms[0])
            if tick + 1 < segments:
                x, low, high = edges_on(out, first, last, [tick])
                skips.append(pass_on(out, [tick], half, 0) if tick + half < segments else None)
        return out.reshape(1, batches, height, columns, channels)

    def pick(array, slot):
        return lax.dynamic_index_in_dim(array, slot, 0, keepdims=False)

    def tick_step(tick, state):
        states, received, skip_buffer = state
        slot = jnp.clip(tick - segment, 0, batches - 1)
        own = pick(flat, slot), pick(low0, slot)[tokens - columns :], pick(high0, slot)[:columns]
        x, low, high = [jnp.where(segment == 0, f, r) for f, r in zip(own, received)]
        out, first, last = section(
            jnp.reshape(tick, (1,)), x, low, high, pick(skip_buffer, slot), pick(states, slot),
            pick(terms, slot),
        )
        states = lax.dynamic_update_index_in_dim(states, out, slot, 0)
        passed = edges_on(out, first, last, range(segments))
        arrived = pass_on(out, range(segments), half, 0)
        partner = tick - segment + half
        fits = (segment >= half) & (partner >= 0) & (partner < batches)
        partner_slot = jnp.clip(partner, 0, batches - 1)
        kept = pick(skip_buffer, partner_slot)
        skip_buffer = lax.dynamic_update_index_in_dim(
            skip_buffer, jnp.where(fits, arrived, kept), partner_slot, 0
        )
        return states, passed, skip_buffer

    edge = jnp.zeros((columns, channels), BF16)
    initial = (jnp.zeros_like(flat), (jnp.zeros_like(flat[0]), edge, edge), jnp.zeros_like(flat))
    states = lax.fori_loop(0, batches + segments - 1, tick_step, initial)[0]
    return states.reshape(1, batches, height, columns, channels)


def solution(mesh):
    return jax.shard_map(
        shards,
        mesh=mesh,
        in_specs=(
            P("groups", "rows", None, None),
            P("groups"),
            P("segment", None, None, None),
            P("segment", None, None, None, None),
            P("segment", None, None),
            P("segment", None, None, None),
            P("segment", None, None, None, None),
            P("segment", None, None, None),
            P("segment", None, None, None),
            P("segment", None, None),
            P("segment", None),
            P("segment"),
            P("segment"),
        ),
        out_specs=P("segment", "groups", "rows", None, None),
        check_vma=False,
    )
```

profile of v0, /device:TPU:29, one launch (start us, length us, event | category | flops | bytes accessed | tf_op | source)
XLA Modules:
  0.0 38.6 jit_solution(4603892657961008899)
XLA Ops:
  0.0 0.7 %collective-permute-start = (bf16[1,128,320]{2,1,0:T(8,128)(2,1)}, bf16[1,128,320]{2,1,0:T(8,128)(2,1)S(1)}, u32[]{:S(2)}, u32[]{:S(2)}) collective-permute-start(bf16[1,128,320]{2,1,0:T(8,128)(2,1)} %bitcast.30), channel_id=1, source_target_pairs={{4,1},{5,2},{6,3},{20,17},{21,18},{22,19}} | collective-permute-start | bytes 245768 | tf_op jit(solution)/shard_map/ppermute | solution.py:453
  0.7 0.7 %collective-permute-start.1 = (bf16[1,128,320]{2,1,0:T(8,128)(2,1)}, bf16[1,128,320]{2,1,0:T(8,128)(2,1)S(1)}, u32[]{:S(2)}, u32[]{:S(2)}) collective-permute-start(bf16[1,128,320]{2,1,0:T(8,128)(2,1)} %bitcast.31), channel_id=1, source_target_pairs={{9,0},{10,1},{11,2},{25,16},{26,17},{27,18}} | collective-permute-start | bytes 245768 | tf_op jit(solution)/shard_map/ppermute | solution.py:453
  3.3 5.5 %weights.1 = (bf16[10,320,320]{2,1,0:T(8,128)(2,1)S(1)}, bf16[320,1024]{1,0:T(8,128)(2,1)S(1)}, bf16[320,320]{1,0:T(8,128)(2,1)S(1)}, bf16[320,1280]{1,0:T(8,128...) custom-call(f32[4,4,4]{2,1,0:T(4,128)} %bitcast.34, ...), custom_call_target="tpu_custom_call" | custom-call | tf_op jit(solution)/shard_map/weights/pallas_call | solution.py:218
  8.8 0.0 collective-permute-done
  8.8 0.0 collective-permute-done.1
  8.8 0.7 %collective-permute-start.2 = (bf16[128,320]{1,0:T(8,128)(2,1)S(1)}, bf16[128,320]{1,0:T(8,128)(2,1)S(1)}, u32[]{:S(2)}, u32[]{:S(2)}) collective-permute-start(bf16[128,320]{1,0:T(8,128)(2,1)S(1)} %get-tuple-element.35.refs_6_), channel_id=1, source_target_pairs={{0,4},{1,5},{2,6},{3,7},{16,20},{17,21},{18,22},{19,23}} | collective-permute-start | bytes 245768 | tf_op jit(solution)/shard_map/ppermute | solution.py:453
  9.5 0.7 %collective-permute-start.3 = (bf16[16,320]{1,0:T(8,128)(2,1)S(1)}, bf16[16,320]{1,0:T(8,128)(2,1)S(1)}, u32[]{:S(2)}, u32[]{:S(2)}) collective-permute-start(bf16[16,320]{1,0:T(8,128)(2,1)S(1)} %get-tuple-element.36), channel_id=1, source_target_pairs={{0,5},{1,6},{2,7},{16,21},{17,22},{18,23}} | collective-permute-start | bytes 30728 | tf_op jit(solution)/shard_map/ppermute | solution.py:453
  10.2 0.7 %collective-permute-start.4 = (bf16[16,320]{1,0:T(8,128)(2,1)S(1)}, bf16[16,320]{1,0:T(8,128)(2,1)S(1)}, u32[]{:S(2)}, u32[]{:S(2)}) collective-permute-start(bf16[16,320]{1,0:T(8,128)(2,1)S(1)} %get-tuple-element.37), channel_id=1, source_target_pairs={{1,4},{2,5},{3,6},{17,20},{18,21},{19,22}} | collective-permute-start | bytes 30728 | tf_op jit(solution)/shard_map/ppermute | solution.py:453
  10.8 0.7 %collective-permute-start.6 = (bf16[128,320]{1,0:T(8,128)(2,1)S(1)}, bf16[128,320]{1,0:T(8,128)(2,1)S(1)}, u32[]{:S(2)}, u32[]{:S(2)}) collective-permute-start(bf16[128,320]{1,0:T(8,128)(2,1)S(1)} %get-tuple-element.35.refs_6_), channel_id=1, source_target_pairs={{0,8},{1,9},{2,10},{3,11},{16,24},{17,25},{18,26},{19,27}} | collective-permute-start | bytes 245768 | tf_op jit(solution)/shard_map/ppermute | solution.py:453
  11.5 0.0 collective-permute-done.2.refs_0_.refs_2_
  11.5 0.0 collective-permute-done.3.refs_4_
  11.6 0.0 collective-permute-done.4.refs_5_
  11.6 0.7 %collective-permute-start.5 = (bf16[128,320]{1,0:T(8,128)(2,1)S(1)}, bf16[128,320]{1,0:T(8,128)(2,1)S(1)}, u32[]{:S(2)}, u32[]{:S(2)}) collective-permute-start(bf16[128,320]{1,0:T(8,128)(2,1)S(1)} %get-tuple-element.38.refs_6_), channel_id=1, source_target_pairs={{4,8},{5,9},{6,10},{7,11},{20,24},{21,25},{22,26},{23,27}} | collective-permute-start | bytes 245768 | tf_op jit(solution)/shard_map/ppermute | solution.py:453
  12.3 0.7 %collective-permute-start.7 = (bf16[16,320]{1,0:T(8,128)(2,1)S(1)}, bf16[16,320]{1,0:T(8,128)(2,1)S(1)}, u32[]{:S(2)}, u32[]{:S(2)}) collective-permute-start(bf16[16,320]{1,0:T(8,128)(2,1)S(1)} %get-tuple-element.39), channel_id=1, source_target_pairs={{4,9},{5,10},{6,11},{20,25},{21,26},{22,27}} | collective-permute-start | bytes 30728 | tf_op jit(solution)/shard_map/ppermute | solution.py:453
  13.0 0.7 %collective-permute-start.8 = (bf16[16,320]{1,0:T(8,128)(2,1)S(1)}, bf16[16,320]{1,0:T(8,128)(2,1)S(1)}, u32[]{:S(2)}, u32[]{:S(2)}) collective-permute-start(bf16[16,320]{1,0:T(8,128)(2,1)S(1)} %get-tuple-element.40), channel_id=1, source_target_pairs={{5,8},{6,9},{7,10},{21,24},{22,25},{23,26}} | collective-permute-start | bytes 30728 | tf_op jit(solution)/shard_map/ppermute | solution.py:453
  13.6 1.3 %collective-permute-start.10 = (bf16[128,320]{1,0:T(8,128)(2,1)S(1)}, bf16[128,320]{1,0:T(8,128)(2,1)S(1)}, u32[]{:S(2)}, u32[]{:S(2)}) collective-permute-start(bf16[128,320]{1,0:T(8,128)(2,1)S(1)} %get-tuple-element.38.refs_6_), channel_id=1, source_target_pairs={{4,12},{5,13},{6,14},{7,15},{20,28},{21,29},{22,30},{23,31}} | collective-permute-start | bytes 245768 | tf_op jit(solution)/shard_map/ppermute | solution.py:453
  14.9 0.0 collective-permute-done.6.refs_0_
  14.9 0.0 collective-permute-done.5.refs_1_.refs_2_
  15.0 0.0 collective-permute-done.7.refs_4_
  15.0 0.0 collective-permute-done.8.refs_5_
  15.0 1.3 %collective-permute-start.9 = (bf16[128,320]{1,0:T(8,128)(2,1)S(1)}, bf16[128,320]{1,0:T(8,128)(2,1)S(1)}, u32[]{:S(2)}, u32[]{:S(2)}) collective-permute-start(bf16[128,320]{1,0:T(8,128)(2,1)S(1)} %get-tuple-element.41.refs_6_), channel_id=1, source_target_pairs={{8,12},{9,13},{10,14},{11,15},{24,28},{25,29},{26,30},{27,31}} | collective-permute-start | bytes 245768 | tf_op jit(solution)/shard_map/ppermute | solution.py:453
  16.3 1.3 %collective-permute-start.11 = (bf16[16,320]{1,0:T(8,128)(2,1)S(1)}, bf16[16,320]{1,0:T(8,128)(2,1)S(1)}, u32[]{:S(2)}, u32[]{:S(2)}) collective-permute-start(bf16[16,320]{1,0:T(8,128)(2,1)S(1)} %get-tuple-element.42), channel_id=1, source_target_pairs={{8,13},{9,14},{10,15},{24,29},{25,30},{26,31}} | collective-permute-start | bytes 30728 | tf_op jit(solution)/shard_map/ppermute | solution.py:453
  17.6 1.3 %collective-permute-start.12 = (bf16[16,320]{1,0:T(8,128)(2,1)S(1)}, bf16[16,320]{1,0:T(8,128)(2,1)S(1)}, u32[]{:S(2)}, u32[]{:S(2)}) collective-permute-start(bf16[16,320]{1,0:T(8,128)(2,1)S(1)} %get-tuple-element.43), channel_id=1, source_target_pairs={{9,12},{10,13},{11,14},{25,28},{26,29},{27,30}} | collective-permute-start | bytes 30728 | tf_op jit(solution)/shard_map/ppermute | solution.py:453
  18.9 10.7 %collective-permute-done.10.refs_0_ = bf16[128,320]{1,0:T(8,128)(2,1)S(1)} collective-permute-done((bf16[128,320]{1,0:T(8,128)(2,1)S(1)}, bf16[128,320]{1,0:T(8,128)(2,1)S(1)}, u32[]{:S(2)}, u32[]{:S(2)}) %collective-permute-start.10) | collective-permute-done | bytes 81952 | tf_op jit(solution)/shard_map/ppermute | solution.py:453
  29.6 3.3 %collective-permute-done.9.refs_1_.refs_2_ = bf16[128,320]{1,0:T(8,128)(2,1)S(1)} collective-permute-done((bf16[128,320]{1,0:T(8,128)(2,1)S(1)}, bf16[128,320]{1,0:T(8,128)(2,1)S(1)}, u32[]{:S(2)}, u32[]{:S(2)}) %collective-permute-start.9) | collective-permute-done | bytes 81952 | tf_op jit(solution)/shard_map/ppermute | solution.py:453
  32.9 0.8 %inner.7.refs_3_ = f32[128,320]{1,0:T(8,128)S(1)} custom-call(bf16[128,320]{1,0:T(8,128)(2,1)S(1)} %collective-permute-done.10.refs_0_, bf16[128,320]{1,0:T(8,128)(2,1)S(1)} %collective-permute-done.9.refs_1_.refs_2_, bf16[10,320,320]{2,1,0:T(8,128)(2,1)S(1)} %get-tuple-element.28.refs_1_.refs_7_.refs_2_, f32[8,320]{1,0:T(8,128)S(1)} %bitcast.22, ...), custom_call_target="tpu_custom_call" | custom-call | tf_op jit(solution)/shard_map/inner/pallas_call | solution.py:400
  33.8 1.2 %collective-permute-done.11.refs_4_ = bf16[16,320]{1,0:T(8,128)(2,1)S(1)} collective-permute-done((bf16[16,320]{1,0:T(8,128)(2,1)S(1)}, bf16[16,320]{1,0:T(8,128)(2,1)S(1)}, u32[]{:S(2)}, u32[]{:S(2)}) %collective-permute-start.11) | collective-permute-done | bytes 10272 | tf_op jit(solution)/shard_map/ppermute | solution.py:453
  35.0 0.7 %collective-permute-done.12.refs_5_ = bf16[16,320]{1,0:T(8,128)(2,1)S(1)} collective-permute-done((bf16[16,320]{1,0:T(8,128)(2,1)S(1)}, bf16[16,320]{1,0:T(8,128)(2,1)S(1)}, u32[]{:S(2)}, u32[]{:S(2)}) %collective-permute-start.12) | collective-permute-done | bytes 10272 | tf_op jit(solution)/shard_map/ppermute | solution.py:453
  35.7 3.0 %outer.7 = (bf16[128,320]{1,0:T(8,128)(2,1)}, bf16[16,320]{1,0:T(8,128)(2,1)}, bf16[16,320]{1,0:T(8,128)(2,1)}) custom-call(s32[2]{0:T(128)S(4)} %get-tuple-element.25.refs_0_, f32[1,5]{1,0:T(1,128)S(4)} %get-tuple-element.26.refs_1_, bf16[128,320]{1,0:T(8,128)(2,1)S(1)} %collective-permute-done.9.refs_1_.refs_2_, f32[128,320]{1,0:T(8,128)S(1)} %inner.7.refs_3_, ...), custom_call_target="tpu_custom_call" | custom-call | tf_op jit(solution)/shard_map/outer/pallas_call | solution.py:419
  (6 shorter events, 0.2 us)
Async XLA Ops:
  0.0 8.8 %collective-permute-start = (bf16[1,128,320]{2,1,0:T(8,128)(2,1)}, bf16[1,128,320]{2,1,0:T(8,128)(2,1)S(1)}, u32[]{:S(2)}, u32[]{:S(2)}) collective-permute-start(bf16[1,128,320]{2,1,0:T(8,128)(2,1)} %bitcast.30), channel_id=1, source_target_pairs={{4,1},{5,2},{6,3},{20,17},{21,18},{22,19}} | collective-permute-start | bytes 245768 | tf_op jit(solution)/shard_map/ppermute | solution.py:453
  0.7 8.1 %collective-permute-start.1 = (bf16[1,128,320]{2,1,0:T(8,128)(2,1)}, bf16[1,128,320]{2,1,0:T(8,128)(2,1)S(1)}, u32[]{:S(2)}, u32[]{:S(2)}) collective-permute-start(bf16[1,128,320]{2,1,0:T(8,128)(2,1)} %bitcast.31), channel_id=1, source_target_pairs={{9,0},{10,1},{11,2},{25,16},{26,17},{27,18}} | collective-permute-start | bytes 245768 | tf_op jit(solution)/shard_map/ppermute | solution.py:453
  8.8 2.7 %collective-permute-start.2 = (bf16[128,320]{1,0:T(8,128)(2,1)S(1)}, bf16[128,320]{1,0:T(8,128)(2,1)S(1)}, u32[]{:S(2)}, u32[]{:S(2)}) collective-permute-start(bf16[128,320]{1,0:T(8,128)(2,1)S(1)} %get-tuple-element.35.refs_6_), channel_id=1, source_target_pairs={{0,4},{1,5},{2,6},{3,7},{16,20},{17,21},{18,22},{19,23}} | collective-permute-start | bytes 245768 | tf_op jit(solution)/shard_map/ppermute | solution.py:453
  9.5 2.1 %collective-permute-start.3 = (bf16[16,320]{1,0:T(8,128)(2,1)S(1)}, bf16[16,320]{1,0:T(8,128)(2,1)S(1)}, u32[]{:S(2)}, u32[]{:S(2)}) collective-permute-start(bf16[16,320]{1,0:T(8,128)(2,1)S(1)} %get-tuple-element.36), channel_id=1, source_target_pairs={{0,5},{1,6},{2,7},{16,21},{17,22},{18,23}} | collective-permute-start | bytes 30728 | tf_op jit(solution)/shard_map/ppermute | solution.py:453
  10.2 1.4 %collective-permute-start.4 = (bf16[16,320]{1,0:T(8,128)(2,1)S(1)}, bf16[16,320]{1,0:T(8,128)(2,1)S(1)}, u32[]{:S(2)}, u32[]{:S(2)}) collective-permute-start(bf16[16,320]{1,0:T(8,128)(2,1)S(1)} %get-tuple-element.37), channel_id=1, source_target_pairs={{1,4},{2,5},{3,6},{17,20},{18,21},{19,22}} | collective-permute-start | bytes 30728 | tf_op jit(solution)/shard_map/ppermute | solution.py:453
  10.8 4.1 %collective-permute-start.6 = (bf16[128,320]{1,0:T(8,128)(2,1)S(1)}, bf16[128,320]{1,0:T(8,128)(2,1)S(1)}, u32[]{:S(2)}, u32[]{:S(2)}) collective-permute-start(bf16[128,320]{1,0:T(8,128)(2,1)S(1)} %get-tuple-element.35.refs_6_), channel_id=1, source_target_pairs={{0,8},{1,9},{2,10},{3,11},{16,24},{17,25},{18,26},{19,27}} | collective-permute-start | bytes 245768 | tf_op jit(solution)/shard_map/ppermute | solution.py:453
  11.6 3.3 %collective-permute-start.5 = (bf16[128,320]{1,0:T(8,128)(2,1)S(1)}, bf16[128,320]{1,0:T(8,128)(2,1)S(1)}, u32[]{:S(2)}, u32[]{:S(2)}) collective-permute-start(bf16[128,320]{1,0:T(8,128)(2,1)S(1)} %get-tuple-element.38.refs_6_), channel_id=1, source_target_pairs={{4,8},{5,9},{6,10},{7,11},{20,24},{21,25},{22,26},{23,27}} | collective-permute-start | bytes 245768 | tf_op jit(solution)/shard_map/ppermute | solution.py:453
  12.3 2.7 %collective-permute-start.7 = (bf16[16,320]{1,0:T(8,128)(2,1)S(1)}, bf16[16,320]{1,0:T(8,128)(2,1)S(1)}, u32[]{:S(2)}, u32[]{:S(2)}) collective-permute-start(bf16[16,320]{1,0:T(8,128)(2,1)S(1)} %get-tuple-element.39), channel_id=1, source_target_pairs={{4,9},{5,10},{6,11},{20,25},{21,26},{22,27}} | collective-permute-start | bytes 30728 | tf_op jit(solution)/shard_map/ppermute | solution.py:453
  13.0 2.0 %collective-permute-start.8 = (bf16[16,320]{1,0:T(8,128)(2,1)S(1)}, bf16[16,320]{1,0:T(8,128)(2,1)S(1)}, u32[]{:S(2)}, u32[]{:S(2)}) collective-permute-start(bf16[16,320]{1,0:T(8,128)(2,1)S(1)} %get-tuple-element.40), channel_id=1, source_target_pairs={{5,8},{6,9},{7,10},{21,24},{22,25},{23,26}} | collective-permute-start | bytes 30728 | tf_op jit(solution)/shard_map/ppermute | solution.py:453
  13.6 16.0 %collective-permute-start.10 = (bf16[128,320]{1,0:T(8,128)(2,1)S(1)}, bf16[128,320]{1,0:T(8,128)(2,1)S(1)}, u32[]{:S(2)}, u32[]{:S(2)}) collective-permute-start(bf16[128,320]{1,0:T(8,128)(2,1)S(1)} %get-tuple-element.38.refs_6_), channel_id=1, source_target_pairs={{4,12},{5,13},{6,14},{7,15},{20,28},{21,29},{22,30},{23,31}} | collective-permute-start | bytes 245768 | tf_op jit(solution)/shard_map/ppermute | solution.py:453
  15.0 17.9 %collective-permute-start.9 = (bf16[128,320]{1,0:T(8,128)(2,1)S(1)}, bf16[128,320]{1,0:T(8,128)(2,1)S(1)}, u32[]{:S(2)}, u32[]{:S(2)}) collective-permute-start(bf16[128,320]{1,0:T(8,128)(2,1)S(1)} %get-tuple-element.41.refs_6_), channel_id=1, source_target_pairs={{8,12},{9,13},{10,14},{11,15},{24,28},{25,29},{26,30},{27,31}} | collective-permute-start | bytes 245768 | tf_op jit(solution)/shard_map/ppermute | solution.py:453
  16.3 18.7 %collective-permute-start.11 = (bf16[16,320]{1,0:T(8,128)(2,1)S(1)}, bf16[16,320]{1,0:T(8,128)(2,1)S(1)}, u32[]{:S(2)}, u32[]{:S(2)}) collective-permute-start(bf16[16,320]{1,0:T(8,128)(2,1)S(1)} %get-tuple-element.42), channel_id=1, source_target_pairs={{8,13},{9,14},{10,15},{24,29},{25,30},{26,31}} | collective-permute-start | bytes 30728 | tf_op jit(solution)/shard_map/ppermute | solution.py:453
  17.6 18.0 %collective-permute-start.12 = (bf16[16,320]{1,0:T(8,128)(2,1)S(1)}, bf16[16,320]{1,0:T(8,128)(2,1)S(1)}, u32[]{:S(2)}, u32[]{:S(2)}) collective-permute-start(bf16[16,320]{1,0:T(8,128)(2,1)S(1)} %get-tuple-element.43), channel_id=1, source_target_pairs={{9,12},{10,13},{11,14},{25,28},{26,29},{27,30}} | collective-permute-start | bytes 30728 | tf_op jit(solution)/shard_map/ppermute | solution.py:453
where the time goes:
time: 38 us; the launch traced here: 38.6 us
  waiting for transfers between devices  15.9 us (42%)
  starting transfers between devices  11.1 us (29%)
  Pallas kernels  9.38 us (25%)
  between operations  2.17 us (6%)
    ppermute x13, waiting for transfers between devices, pass_on(): return lax.ppermute(value, axes, links)  15.9 us
    ppermute x13, starting transfers between devices, pass_on(): return lax.ppermute(value, axes, links)  11.1 us
    pallas_call x1, Pallas kernels, section_weights(): pl.pallas_call(functools.partial(weights_kernel, first_skip), out_shape=(...  5.46 us
    pallas_call x4, Pallas kernels, run_outer(): pl.pallas_call(functools.partial(outer_kernel, columns, tick if static el...  3.05 us
    pallas_call x4, Pallas kernels, run_inner(): pl.pallas_call(functools.partial(inner_kernel, columns, tick if static el...  0.88 us
  transfers between devices with their start and end apart: 13, of which 4 were waited for; matrix products, arithmetic and copies ran while one was open for 0% of the time, Pallas kernels for 17%

commit v1 on v0

--- a/solution.py
+++ b/solution.py
@@ -60,7 +60,7 @@
     mix_out, qkv_out, out_out, up_out, down_out, term_out, gain_out, meta_out, scale_out,
     hidden_out,
     rule_ref, time_ref, flag_ref, offset_ref, conv_ref, attn_ref, up_ref, down_ref,
-    skip_ref, proj_ref, rows_ref, sems,
+    skip_ref, proj_ref, rows_ref, pair_ref, sems,
 ):
     sources = [
         rule_hbm, conv_hbm, skip_hbm, time_hbm, proj_hbm, flag_hbm, offset_hbm, scale_hbm,
@@ -81,15 +81,6 @@
     def rule(i, a, b):
         return rule_ref[i, a, b]
 
-    def block_row(factors, a):
-        blocks = []
-        for b in range(QUAT):
-            total = factors[0] * rule(0, a, b)
-            for i in range(1, QUAT):
-                total = total + factors[i] * rule(i, a, b)
-            blocks.append(total)
-        return blocks
-
     channels = proj_ref.shape[0]
     tail = channels % LANES
     full = channels - tail
@@ -108,12 +99,28 @@
             row = jnp.where(block == 0, rule(i, a, 0), rule(i, a, 1))
             row = jnp.where(block == 2, rule(i, a, 2), row)
             rows_ref[i * QUAT + a] = jnp.where(block == 3, rule(i, a, 3), row)
-
-    def square(factors, store):
+    on_left = lax.broadcasted_iota(jnp.int32, (8, LANES), 1) < tail
+    for place in range(QUAT * QUAT // 2):
+        left, right = rows_ref[2 * place, :, full:], rows_ref[2 * place + 1, :, full:]
+        pair_ref[place] = jnp.where(on_left, left, right)
+
+    def combine(parts, scales):
+        total = parts[0] * scales[0]
+        for value, scale in zip(parts[1:], scales[1:]):
+            total = total + value * scale
+        return total
+
+    def square(factors, store, keep_right=False):
         stacked = factors.reshape(QUAT * part, part)
         for tile in range(padded // LANES):
             at = slice(tile * LANES, (tile + 1) * LANES)
-            rows = [rows_ref[place, :, at][None] for place in range(QUAT * QUAT)]
+            halves = tile * LANES == full
+            if halves:
+                rows = [pair_ref[place][None] for place in range(QUAT * QUAT // 2)]
+            else:
+                rows = [rows_ref[place, :, at][None] for place in range(QUAT * QUAT)]
+            step = 2 if halves else 1
+            groups = QUAT // step
             whole = dot(stacked, repeat[:, at])
             for chunk in range(part // 16):
                 spread = [
@@ -121,12 +128,17 @@
                     for i in range(QUAT)
                 ]
                 spread = [value.reshape(2, 8, LANES) for value in spread]
-                for a in range(QUAT):
-                    total = spread[0] * rows[a]
-                    for i in range(1, QUAT):
-                        total = total + spread[i] * rows[i * QUAT + a]
-                    start = a * part + chunk * 16
-                    store(tile, slice(start, start + 16), total.reshape(16, LANES).astype(BF16))
+                for group in range(groups):
+                    scales = [rows[i * groups + group] for i in range(QUAT)]
+                    total = combine(spread, scales).reshape(16, LANES)
+                    values = [total]
+                    if halves:
+                        values.append(pltpu.roll(total, tail, 1))
+                        if keep_right:
+                            values.reverse()
+                    for place, value in enumerate(values):
+                        start = (group * step + place) * part + chunk * 16
+                        store(tile, slice(start, start + 16), value.astype(BF16))
 
     def store_plain(out):
         def store(tile, rows, value):
@@ -173,34 +185,37 @@
     @pl.when(flag_ref[0] == 1)
     def _():
         for which in range(3):
-            square(attn_ref[which], store_heads(which))
+            square(attn_ref[which], store_heads(which), which == 1)
         square(attn_ref[3], store_plain(out_out))
-
-        def store_wide(out, place, rows, value):
-            out[rows, place * full : (place + 1) * full] = value[:, :full].astype(BF16)
-            at, low = QUAT * full + place // 2 * LANES, place % 2 * tail
-            half_tile = value[:, full + low : full + low + tail].astype(BF16)
-            out[rows, at + low : at + low + tail] = half_tile
 
         def widen(value):
             value = value.astype(F32)
-            return jnp.concatenate([value, value[:, full:]], axis=1)
+            return value[:, :full], jnp.concatenate([value[:, full:]] * 2, axis=1)
+
+        def wide_block(factors, out, rows, fixed, place_of):
+            for place in range(QUAT):
+                scales = [rule(i, *place_of(fixed, place)) for i in range(QUAT)]
+                value = combine([whole for whole, _ in factors], scales)
+                out[rows, place * full : (place + 1) * full] = value.astype(BF16)
+            for pair in range(QUAT // 2):
+                scales = []
+                for i in range(QUAT):
+                    left = rule(i, *place_of(fixed, 2 * pair))
+                    right = rule(i, *place_of(fixed, 2 * pair + 1))
+                    scales.append(jnp.where(on_left, left, right)[None])
+                halves = [half.reshape(2, 8, LANES) for _, half in factors]
+                value = combine(halves, scales).reshape(16, LANES)
+                at = QUAT * full + pair * LANES
+                out[rows, at : at + LANES] = value.astype(BF16)
 
         def wide_step(chunk, carry):
             start = pl.multiple_of(chunk * 16, 16)
             ups = [widen(up_ref[i, pl.ds(start, 16), :]) for i in range(QUAT)]
             downs = [widen(down_ref[i, pl.ds(start, 16), :]) for i in range(QUAT)]
-            for a in range(QUAT):
-                rows = pl.ds(pl.multiple_of(a * part + start, 16), 16)
-                for b, value in enumerate(block_row(ups, a)):
-                    store_wide(up_out, b, rows, value)
-            for b in range(QUAT):
-                rows = pl.ds(pl.multiple_of(b * part + start, 16), 16)
-                for a in range(QUAT):
-                    total = downs[0] * rule(0, a, b)
-                    for i in range(1, QUAT):
-                        total = total + downs[i] * rule(i, a, b)
-                    store_wide(down_out, a, rows, total)
+            for fixed in range(QUAT):
+                rows = pl.ds(pl.multiple_of(fixed * part + start, 16), 16)
+                wide_block(ups, up_out, rows, fixed, lambda a, b: (a, b))
+                wide_block(downs, down_out, rows, fixed, lambda b, a: (a, b))
             return carry
 
         lax.fori_loop(0, part // 16, wide_step, 0)
@@ -240,6 +255,7 @@
         + [pltpu.VMEM(array.shape, BF16) for array in (conv, attn, up, down, skip, proj)]
         + [
             pltpu.VMEM((QUAT * QUAT, 8, padded), F32),
+            pltpu.VMEM((QUAT * QUAT // 2, 8, LANES), F32),
             pltpu.SemaphoreType.DMA((len(operands),)),
         ],
         compiler_params=pltpu.CompilerParams(vmem_limit_bytes=12 * MIB),

time: 38 us -> 36.6 us (0.963); the launches traced: 38.6 us -> 36.3 us
  waiting for transfers between devices: 15.9 us -> 14 us
  Pallas kernels: 9.38 us -> 8.94 us
    ppermute x13, waiting for transfers between devices: 15.9 us -> 14 us  [pass_on(): return lax.ppermute(value, axes, links)]
    pallas_call x1, Pallas kernels: 5.46 us -> 5.02 us  [section_weights(): pl.pallas_call(functools.partial(weights_kernel, first_skip), out_shape=(...]
  transfers between devices with their start and end apart: 13 -> 13, of which waited for: 4 -> 4; matrix products, arithmetic and copies ran while one was open for 0% -> 0% of each run, Pallas kernels for 17% -> 16%
where the time goes in v1:
time: 36.6 us; the launch traced here: 36.3 us
  waiting for transfers between devices  14 us (38%)
  starting transfers between devices  11.1 us (30%)
  Pallas kernels  8.94 us (24%)
  between operations  2.17 us (6%)
    ppermute x13, waiting for transfers between devices, pass_on(): return lax.ppermute(value, axes, links)  14 us
    ppermute x13, starting transfers between devices, pass_on(): return lax.ppermute(value, axes, links)  11.1 us
    pallas_call x1, Pallas kernels, section_weights(): pl.pallas_call(functools.partial(weights_kernel, first_skip), out_shape=(...  5.02 us
    pallas_call x4, Pallas kernels, run_outer(): pl.pallas_call(functools.partial(outer_kernel, columns, tick if static el...  3.05 us
    pallas_call x4, Pallas kernels, run_inner(): pl.pallas_call(functools.partial(inner_kernel, columns, tick if static el...  0.88 us
  transfers between devices with their start and end apart: 13, of which 4 were waited for; matrix products, arithmetic and copies ran while one was open for 0% of the time, Pallas kernels for 16%

profile of v1, /device:TPU:29, one launch (start us, length us, event | category | flops | bytes accessed | tf_op | source)
XLA Modules:
  0.0 36.3 jit_solution(6727949307472802502)
XLA Ops:
  0.0 0.7 %collective-permute-start = (bf16[1,128,320]{2,1,0:T(8,128)(2,1)}, bf16[1,128,320]{2,1,0:T(8,128)(2,1)S(1)}, u32[]{:S(2)}, u32[]{:S(2)}) collective-permute-start(bf16[1,128,320]{2,1,0:T(8,128)(2,1)} %bitcast.30), channel_id=1, source_target_pairs={{4,1},{5,2},{6,3},{20,17},{21,18},{22,19}} | collective-permute-start | bytes 245768 | tf_op jit(solution)/shard_map/ppermute | solution.py:469
  0.7 0.7 %collective-permute-start.1 = (bf16[1,128,320]{2,1,0:T(8,128)(2,1)}, bf16[1,128,320]{2,1,0:T(8,128)(2,1)S(1)}, u32[]{:S(2)}, u32[]{:S(2)}) collective-permute-start(bf16[1,128,320]{2,1,0:T(8,128)(2,1)} %bitcast.31), channel_id=1, source_target_pairs={{9,0},{10,1},{11,2},{25,16},{26,17},{27,18}} | collective-permute-start | bytes 245768 | tf_op jit(solution)/shard_map/ppermute | solution.py:469
  3.3 5.0 %weights.1 = (bf16[10,320,320]{2,1,0:T(8,128)(2,1)S(1)}, bf16[320,1024]{1,0:T(8,128)(2,1)S(1)}, bf16[320,320]{1,0:T(8,128)(2,1)S(1)}, bf16[320,1280]{1,0:T(8,128...) custom-call(f32[4,4,4]{2,1,0:T(4,128)} %bitcast.34, ...), custom_call_target="tpu_custom_call" | custom-call | tf_op jit(solution)/shard_map/weights/pallas_call | solution.py:233
  8.3 0.0 collective-permute-done
  8.3 0.0 collective-permute-done.1
  8.4 0.7 %collective-permute-start.2 = (bf16[128,320]{1,0:T(8,128)(2,1)S(1)}, bf16[128,320]{1,0:T(8,128)(2,1)S(1)}, u32[]{:S(2)}, u32[]{:S(2)}) collective-permute-start(bf16[128,320]{1,0:T(8,128)(2,1)S(1)} %get-tuple-element.35.refs_6_), channel_id=1, source_target_pairs={{0,4},{1,5},{2,6},{3,7},{16,20},{17,21},{18,22},{19,23}} | collective-permute-start | bytes 245768 | tf_op jit(solution)/shard_map/ppermute | solution.py:469
  9.1 0.7 %collective-permute-start.3 = (bf16[16,320]{1,0:T(8,128)(2,1)S(1)}, bf16[16,320]{1,0:T(8,128)(2,1)S(1)}, u32[]{:S(2)}, u32[]{:S(2)}) collective-permute-start(bf16[16,320]{1,0:T(8,128)(2,1)S(1)} %get-tuple-element.36), channel_id=1, source_target_pairs={{0,5},{1,6},{2,7},{16,21},{17,22},{18,23}} | collective-permute-start | bytes 30728 | tf_op jit(solution)/shard_map/ppermute | solution.py:469
  9.7 0.7 %collective-permute-start.4 = (bf16[16,320]{1,0:T(8,128)(2,1)S(1)}, bf16[16,320]{1,0:T(8,128)(2,1)S(1)}, u32[]{:S(2)}, u32[]{:S(2)}) collective-permute-start(bf16[16,320]{1,0:T(8,128)(2,1)S(1)} %get-tuple-element.37), channel_id=1, source_target_pairs={{1,4},{2,5},{3,6},{17,20},{18,21},{19,22}} | collective-permute-start | bytes 30728 | tf_op jit(solution)/shard_map/ppermute | solution.py:469
  10.4 0.7 %collective-permute-start.6 = (bf16[128,320]{1,0:T(8,128)(2,1)S(1)}, bf16[128,320]{1,0:T(8,128)(2,1)S(1)}, u32[]{:S(2)}, u32[]{:S(2)}) collective-permute-start(bf16[128,320]{1,0:T(8,128)(2,1)S(1)} %get-tuple-element.35.refs_6_), channel_id=1, source_target_pairs={{0,8},{1,9},{2,10},{3,11},{16,24},{17,25},{18,26},{19,27}} | collective-permute-start | bytes 245768 | tf_op jit(solution)/shard_map/ppermute | solution.py:469
  11.1 0.0 collective-permute-done.2.refs_0_.refs_2_
  11.1 0.0 collective-permute-done.3.refs_4_
  11.1 0.0 collective-permute-done.4.refs_5_
  11.2 0.7 %collective-permute-start.5 = (bf16[128,320]{1,0:T(8,128)(2,1)S(1)}, bf16[128,320]{1,0:T(8,128)(2,1)S(1)}, u32[]{:S(2)}, u32[]{:S(2)}) collective-permute-start(bf16[128,320]{1,0:T(8,128)(2,1)S(1)} %get-tuple-element.38.refs_6_), channel_id=1, source_target_pairs={{4,8},{5,9},{6,10},{7,11},{20,24},{21,25},{22,26},{23,27}} | collective-permute-start | bytes 245768 | tf_op jit(solution)/shard_map/ppermute | solution.py:469
  11.8 0.7 %collective-permute-start.7 = (bf16[16,320]{1,0:T(8,128)(2,1)S(1)}, bf16[16,320]{1,0:T(8,128)(2,1)S(1)}, u32[]{:S(2)}, u32[]{:S(2)}) collective-permute-start(bf16[16,320]{1,0:T(8,128)(2,1)S(1)} %get-tuple-element.39), channel_id=1, source_target_pairs={{4,9},{5,10},{6,11},{20,25},{21,26},{22,27}} | collective-permute-start | bytes 30728 | tf_op jit(solution)/shard_map/ppermute | solution.py:469
  12.5 0.7 %collective-permute-start.8 = (bf16[16,320]{1,0:T(8,128)(2,1)S(1)}, bf16[16,320]{1,0:T(8,128)(2,1)S(1)}, u32[]{:S(2)}, u32[]{:S(2)}) collective-permute-start(bf16[16,320]{1,0:T(8,128)(2,1)S(1)} %get-tuple-element.40), channel_id=1, source_target_pairs={{5,8},{6,9},{7,10},{21,24},{22,25},{23,26}} | collective-permute-start | bytes 30728 | tf_op jit(solution)/shard_map/ppermute | solution.py:469
  13.2 1.3 %collective-permute-start.10 = (bf16[128,320]{1,0:T(8,128)(2,1)S(1)}, bf16[128,320]{1,0:T(8,128)(2,1)S(1)}, u32[]{:S(2)}, u32[]{:S(2)}) collective-permute-start(bf16[128,320]{1,0:T(8,128)(2,1)S(1)} %get-tuple-element.38.refs_6_), channel_id=1, source_target_pairs={{4,12},{5,13},{6,14},{7,15},{20,28},{21,29},{22,30},{23,31}} | collective-permute-start | bytes 245768 | tf_op jit(solution)/shard_map/ppermute | solution.py:469
  14.5 0.0 collective-permute-done.6.refs_0_
  14.5 0.0 collective-permute-done.5.refs_1_.refs_2_
  14.5 0.0 collective-permute-done.7.refs_4_
  14.5 0.0 collective-permute-done.8.refs_5_
  14.6 1.3 %collective-permute-start.9 = (bf16[128,320]{1,0:T(8,128)(2,1)S(1)}, bf16[128,320]{1,0:T(8,128)(2,1)S(1)}, u32[]{:S(2)}, u32[]{:S(2)}) collective-permute-start(bf16[128,320]{1,0:T(8,128)(2,1)S(1)} %get-tuple-element.41.refs_6_), channel_id=1, source_target_pairs={{8,12},{9,13},{10,14},{11,15},{24,28},{25,29},{26,30},{27,31}} | collective-permute-start | bytes 245768 | tf_op jit(solution)/shard_map/ppermute | solution.py:469
  15.9 1.3 %collective-permute-start.11 = (bf16[16,320]{1,0:T(8,128)(2,1)S(1)}, bf16[16,320]{1,0:T(8,128)(2,1)S(1)}, u32[]{:S(2)}, u32[]{:S(2)}) collective-permute-start(bf16[16,320]{1,0:T(8,128)(2,1)S(1)} %get-tuple-element.42), channel_id=1, source_target_pairs={{8,13},{9,14},{10,15},{24,29},{25,30},{26,31}} | collective-permute-start | bytes 30728 | tf_op jit(solution)/shard_map/ppermute | solution.py:469
  17.2 1.3 %collective-permute-start.12 = (bf16[16,320]{1,0:T(8,128)(2,1)S(1)}, bf16[16,320]{1,0:T(8,128)(2,1)S(1)}, u32[]{:S(2)}, u32[]{:S(2)}) collective-permute-start(bf16[16,320]{1,0:T(8,128)(2,1)S(1)} %get-tuple-element.43), channel_id=1, source_target_pairs={{9,12},{10,13},{11,14},{25,28},{26,29},{27,30}} | collective-permute-start | bytes 30728 | tf_op jit(solution)/shard_map/ppermute | solution.py:469
  18.5 10.6 %collective-permute-done.10.refs_0_ = bf16[128,320]{1,0:T(8,128)(2,1)S(1)} collective-permute-done((bf16[128,320]{1,0:T(8,128)(2,1)S(1)}, bf16[128,320]{1,0:T(8,128)(2,1)S(1)}, u32[]{:S(2)}, u32[]{:S(2)}) %collective-permute-start.10) | collective-permute-done | bytes 81952 | tf_op jit(solution)/shard_map/ppermute | solution.py:469
  29.1 1.7 %collective-permute-done.9.refs_1_.refs_2_ = bf16[128,320]{1,0:T(8,128)(2,1)S(1)} collective-permute-done((bf16[128,320]{1,0:T(8,128)(2,1)S(1)}, bf16[128,320]{1,0:T(8,128)(2,1)S(1)}, u32[]{:S(2)}, u32[]{:S(2)}) %collective-permute-start.9) | collective-permute-done | bytes 81952 | tf_op jit(solution)/shard_map/ppermute | solution.py:469
  30.8 0.8 %inner.7.refs_3_ = f32[128,320]{1,0:T(8,128)S(1)} custom-call(bf16[128,320]{1,0:T(8,128)(2,1)S(1)} %collective-permute-done.10.refs_0_, bf16[128,320]{1,0:T(8,128)(2,1)S(1)} %collective-permute-done.9.refs_1_.refs_2_, bf16[10,320,320]{2,1,0:T(8,128)(2,1)S(1)} %get-tuple-element.28.refs_1_.refs_7_.refs_2_, f32[8,320]{1,0:T(8,128)S(1)} %bitcast.22, ...), custom_call_target="tpu_custom_call" | custom-call | tf_op jit(solution)/shard_map/inner/pallas_call | solution.py:416
  31.6 0.7 %collective-permute-done.11.refs_4_ = bf16[16,320]{1,0:T(8,128)(2,1)S(1)} collective-permute-done((bf16[16,320]{1,0:T(8,128)(2,1)S(1)}, bf16[16,320]{1,0:T(8,128)(2,1)S(1)}, u32[]{:S(2)}, u32[]{:S(2)}) %collective-permute-start.11) | collective-permute-done | bytes 10272 | tf_op jit(solution)/shard_map/ppermute | solution.py:469
  32.3 1.0 %collective-permute-done.12.refs_5_ = bf16[16,320]{1,0:T(8,128)(2,1)S(1)} collective-permute-done((bf16[16,320]{1,0:T(8,128)(2,1)S(1)}, bf16[16,320]{1,0:T(8,128)(2,1)S(1)}, u32[]{:S(2)}, u32[]{:S(2)}) %collective-permute-start.12) | collective-permute-done | bytes 10272 | tf_op jit(solution)/shard_map/ppermute | solution.py:469
  33.4 2.9 %outer.7 = (bf16[128,320]{1,0:T(8,128)(2,1)}, bf16[16,320]{1,0:T(8,128)(2,1)}, bf16[16,320]{1,0:T(8,128)(2,1)}) custom-call(s32[2]{0:T(128)S(4)} %get-tuple-element.25.refs_0_, f32[1,5]{1,0:T(1,128)S(4)} %get-tuple-element.26.refs_1_, bf16[128,320]{1,0:T(8,128)(2,1)S(1)} %collective-permute-done.9.refs_1_.refs_2_, f32[128,320]{1,0:T(8,128)S(1)} %inner.7.refs_3_, ...), custom_call_target="tpu_custom_call" | custom-call | tf_op jit(solution)/shard_map/outer/pallas_call | solution.py:435
  (6 shorter events, 0.2 us)
Async XLA Ops:
  0.0 8.3 %collective-permute-start = (bf16[1,128,320]{2,1,0:T(8,128)(2,1)}, bf16[1,128,320]{2,1,0:T(8,128)(2,1)S(1)}, u32[]{:S(2)}, u32[]{:S(2)}) collective-permute-start(bf16[1,128,320]{2,1,0:T(8,128)(2,1)} %bitcast.30), channel_id=1, source_target_pairs={{4,1},{5,2},{6,3},{20,17},{21,18},{22,19}} | collective-permute-start | bytes 245768 | tf_op jit(solution)/shard_map/ppermute | solution.py:469
  0.7 7.7 %collective-permute-start.1 = (bf16[1,128,320]{2,1,0:T(8,128)(2,1)}, bf16[1,128,320]{2,1,0:T(8,128)(2,1)S(1)}, u32[]{:S(2)}, u32[]{:S(2)}) collective-permute-start(bf16[1,128,320]{2,1,0:T(8,128)(2,1)} %bitcast.31), channel_id=1, source_target_pairs={{9,0},{10,1},{11,2},{25,16},{26,17},{27,18}} | collective-permute-start | bytes 245768 | tf_op jit(solution)/shard_map/ppermute | solution.py:469
  8.4 2.7 %collective-permute-start.2 = (bf16[128,320]{1,0:T(8,128)(2,1)S(1)}, bf16[128,320]{1,0:T(8,128)(2,1)S(1)}, u32[]{:S(2)}, u32[]{:S(2)}) collective-permute-start(bf16[128,320]{1,0:T(8,128)(2,1)S(1)} %get-tuple-element.35.refs_6_), channel_id=1, source_target_pairs={{0,4},{1,5},{2,6},{3,7},{16,20},{17,21},{18,22},{19,23}} | collective-permute-start | bytes 245768 | tf_op jit(solution)/shard_map/ppermute | solution.py:469
  9.1 2.1 %collective-permute-start.3 = (bf16[16,320]{1,0:T(8,128)(2,1)S(1)}, bf16[16,320]{1,0:T(8,128)(2,1)S(1)}, u32[]{:S(2)}, u32[]{:S(2)}) collective-permute-start(bf16[16,320]{1,0:T(8,128)(2,1)S(1)} %get-tuple-element.36), channel_id=1, source_target_pairs={{0,5},{1,6},{2,7},{16,21},{17,22},{18,23}} | collective-permute-start | bytes 30728 | tf_op jit(solution)/shard_map/ppermute | solution.py:469
  9.7 1.4 %collective-permute-start.4 = (bf16[16,320]{1,0:T(8,128)(2,1)S(1)}, bf16[16,320]{1,0:T(8,128)(2,1)S(1)}, u32[]{:S(2)}, u32[]{:S(2)}) collective-permute-start(bf16[16,320]{1,0:T(8,128)(2,1)S(1)} %get-tuple-element.37), channel_id=1, source_target_pairs={{1,4},{2,5},{3,6},{17,20},{18,21},{19,22}} | collective-permute-start | bytes 30728 | tf_op jit(solution)/shard_map/ppermute | solution.py:469
  10.4 4.1 %collective-permute-start.6 = (bf16[128,320]{1,0:T(8,128)(2,1)S(1)}, bf16[128,320]{1,0:T(8,128)(2,1)S(1)}, u32[]{:S(2)}, u32[]{:S(2)}) collective-permute-start(bf16[128,320]{1,0:T(8,128)(2,1)S(1)} %get-tuple-element.35.refs_6_), channel_id=1, source_target_pairs={{0,8},{1,9},{2,10},{3,11},{16,24},{17,25},{18,26},{19,27}} | collective-permute-start | bytes 245768 | tf_op jit(solution)/shard_map/ppermute | solution.py:469
  11.2 3.3 %collective-permute-start.5 = (bf16[128,320]{1,0:T(8,128)(2,1)S(1)}, bf16[128,320]{1,0:T(8,128)(2,1)S(1)}, u32[]{:S(2)}, u32[]{:S(2)}) collective-permute-start(bf16[128,320]{1,0:T(8,128)(2,1)S(1)} %get-tuple-element.38.refs_6_), channel_id=1, source_target_pairs={{4,8},{5,9},{6,10},{7,11},{20,24},{21,25},{22,26},{23,27}} | collective-permute-start | bytes 245768 | tf_op jit(solution)/shard_map/ppermute | solution.py:469
  11.8 2.7 %collective-permute-start.7 = (bf16[16,320]{1,0:T(8,128)(2,1)S(1)}, bf16[16,320]{1,0:T(8,128)(2,1)S(1)}, u32[]{:S(2)}, u32[]{:S(2)}) collective-permute-start(bf16[16,320]{1,0:T(8,128)(2,1)S(1)} %get-tuple-element.39), channel_id=1, source_target_pairs={{4,9},{5,10},{6,11},{20,25},{21,26},{22,27}} | collective-permute-start | bytes 30728 | tf_op jit(solution)/shard_map/ppermute | solution.py:469
  12.5 2.0 %collective-permute-start.8 = (bf16[16,320]{1,0:T(8,128)(2,1)S(1)}, bf16[16,320]{1,0:T(8,128)(2,1)S(1)}, u32[]{:S(2)}, u32[]{:S(2)}) collective-permute-start(bf16[16,320]{1,0:T(8,128)(2,1)S(1)} %get-tuple-element.40), channel_id=1, source_target_pairs={{5,8},{6,9},{7,10},{21,24},{22,25},{23,26}} | collective-permute-start | bytes 30728 | tf_op jit(solution)/shard_map/ppermute | solution.py:469
  13.2 15.9 %collective-permute-start.10 = (bf16[128,320]{1,0:T(8,128)(2,1)S(1)}, bf16[128,320]{1,0:T(8,128)(2,1)S(1)}, u32[]{:S(2)}, u32[]{:S(2)}) collective-permute-start(bf16[128,320]{1,0:T(8,128)(2,1)S(1)} %get-tuple-element.38.refs_6_), channel_id=1, source_target_pairs={{4,12},{5,13},{6,14},{7,15},{20,28},{21,29},{22,30},{23,31}} | collective-permute-start | bytes 245768 | tf_op jit(solution)/shard_map/ppermute | solution.py:469
  14.6 16.2 %collective-permute-start.9 = (bf16[128,320]{1,0:T(8,128)(2,1)S(1)}, bf16[128,320]{1,0:T(8,128)(2,1)S(1)}, u32[]{:S(2)}, u32[]{:S(2)}) collective-permute-start(bf16[128,320]{1,0:T(8,128)(2,1)S(1)} %get-tuple-element.41.refs_6_), channel_id=1, source_target_pairs={{8,12},{9,13},{10,14},{11,15},{24,28},{25,29},{26,30},{27,31}} | collective-permute-start | bytes 245768 | tf_op jit(solution)/shard_map/ppermute | solution.py:469
  15.9 16.4 %collective-permute-start.11 = (bf16[16,320]{1,0:T(8,128)(2,1)S(1)}, bf16[16,320]{1,0:T(8,128)(2,1)S(1)}, u32[]{:S(2)}, u32[]{:S(2)}) collective-permute-start(bf16[16,320]{1,0:T(8,128)(2,1)S(1)} %get-tuple-element.42), channel_id=1, source_target_pairs={{8,13},{9,14},{10,15},{24,29},{25,30},{26,31}} | collective-permute-start | bytes 30728 | tf_op jit(solution)/shard_map/ppermute | solution.py:469
  17.2 16.2 %collective-permute-start.12 = (bf16[16,320]{1,0:T(8,128)(2,1)S(1)}, bf16[16,320]{1,0:T(8,128)(2,1)S(1)}, u32[]{:S(2)}, u32[]{:S(2)}) collective-permute-start(bf16[16,320]{1,0:T(8,128)(2,1)S(1)} %get-tuple-element.43), channel_id=1, source_target_pairs={{9,12},{10,13},{11,14},{25,28},{26,29},{27,30}} | collective-permute-start | bytes 30728 | tf_op jit(solution)/shard_map/ppermute | solution.py:469

commit v2 on v1

--- a/solution.py
+++ b/solution.py
@@ -218,7 +218,7 @@
                 wide_block(downs, down_out, rows, fixed, lambda b, a: (a, b))
             return carry
 
-        lax.fori_loop(0, part // 16, wide_step, 0)
+        lax.fori_loop(0, part // 16, wide_step, 0, unroll=True)
 
 
 def section_weights(

time: 36.6 us -> 35.6 us (0.973); the launches traced: 36.3 us -> 36.1 us
  no operation moved by 1% of the time
where the time goes in v2:
time: 35.6 us; the launch traced here: 36.1 us
  waiting for transfers between devices  14 us (39%)
  starting transfers between devices  11.1 us (31%)
  Pallas kernels  8.82 us (25%)
  between operations  2.17 us (6%)
    ppermute x13, waiting for transfers between devices, pass_on(): return lax.ppermute(value, axes, links)  14 us
    ppermute x13, starting transfers between devices, pass_on(): return lax.ppermute(value, axes, links)  11.1 us
    pallas_call x1, Pallas kernels, section_weights(): pl.pallas_call(functools.partial(weights_kernel, first_skip), out_shape=(...  4.89 us
    pallas_call x4, Pallas kernels, run_outer(): pl.pallas_call(functools.partial(outer_kernel, columns, tick if static el...  3.05 us
    pallas_call x4, Pallas kernels, run_inner(): pl.pallas_call(functools.partial(inner_kernel, columns, tick if static el...  0.88 us
  transfers between devices with their start and end apart: 13, of which 4 were waited for; matrix products, arithmetic and copies ran while one was open for 0% of the time, Pallas kernels for 16%

profile of v2, /device:TPU:29, one launch (start us, length us, event | category | flops | bytes accessed | tf_op | source)
XLA Modules:
  0.0 36.1 jit_solution(14158027318305058509)
XLA Ops:
  0.0 0.7 %collective-permute-start = (bf16[1,128,320]{2,1,0:T(8,128)(2,1)}, bf16[1,128,320]{2,1,0:T(8,128)(2,1)S(1)}, u32[]{:S(2)}, u32[]{:S(2)}) collective-permute-start(bf16[1,128,320]{2,1,0:T(8,128)(2,1)} %bitcast.30), channel_id=1, source_target_pairs={{4,1},{5,2},{6,3},{20,17},{21,18},{22,19}} | collective-permute-start | bytes 245768 | tf_op jit(solution)/shard_map/ppermute | solution.py:469
  0.7 0.7 %collective-permute-start.1 = (bf16[1,128,320]{2,1,0:T(8,128)(2,1)}, bf16[1,128,320]{2,1,0:T(8,128)(2,1)S(1)}, u32[]{:S(2)}, u32[]{:S(2)}) collective-permute-start(bf16[1,128,320]{2,1,0:T(8,128)(2,1)} %bitcast.31), channel_id=1, source_target_pairs={{9,0},{10,1},{11,2},{25,16},{26,17},{27,18}} | collective-permute-start | bytes 245768 | tf_op jit(solution)/shard_map/ppermute | solution.py:469
  3.3 4.9 %weights.1 = (bf16[10,320,320]{2,1,0:T(8,128)(2,1)S(1)}, bf16[320,1024]{1,0:T(8,128)(2,1)S(1)}, bf16[320,320]{1,0:T(8,128)(2,1)S(1)}, bf16[320,1280]{1,0:T(8,128...) custom-call(f32[4,4,4]{2,1,0:T(4,128)} %bitcast.34, ...), custom_call_target="tpu_custom_call" | custom-call | tf_op jit(solution)/shard_map/weights/pallas_call | solution.py:233
  8.2 0.0 collective-permute-done
  8.2 0.0 collective-permute-done.1
  8.3 0.7 %collective-permute-start.2 = (bf16[128,320]{1,0:T(8,128)(2,1)S(1)}, bf16[128,320]{1,0:T(8,128)(2,1)S(1)}, u32[]{:S(2)}, u32[]{:S(2)}) collective-permute-start(bf16[128,320]{1,0:T(8,128)(2,1)S(1)} %get-tuple-element.35.refs_6_), channel_id=1, source_target_pairs={{0,4},{1,5},{2,6},{3,7},{16,20},{17,21},{18,22},{19,23}} | collective-permute-start | bytes 245768 | tf_op jit(solution)/shard_map/ppermute | solution.py:469
  8.9 0.7 %collective-permute-start.3 = (bf16[16,320]{1,0:T(8,128)(2,1)S(1)}, bf16[16,320]{1,0:T(8,128)(2,1)S(1)}, u32[]{:S(2)}, u32[]{:S(2)}) collective-permute-start(bf16[16,320]{1,0:T(8,128)(2,1)S(1)} %get-tuple-element.36), channel_id=1, source_target_pairs={{0,5},{1,6},{2,7},{16,21},{17,22},{18,23}} | collective-permute-start | bytes 30728 | tf_op jit(solution)/shard_map/ppermute | solution.py:469
  9.6 0.7 %collective-permute-start.4 = (bf16[16,320]{1,0:T(8,128)(2,1)S(1)}, bf16[16,320]{1,0:T(8,128)(2,1)S(1)}, u32[]{:S(2)}, u32[]{:S(2)}) collective-permute-start(bf16[16,320]{1,0:T(8,128)(2,1)S(1)} %get-tuple-element.37), channel_id=1, source_target_pairs={{1,4},{2,5},{3,6},{17,20},{18,21},{19,22}} | collective-permute-start | bytes 30728 | tf_op jit(solution)/shard_map/ppermute | solution.py:469
  10.3 0.7 %collective-permute-start.6 = (bf16[128,320]{1,0:T(8,128)(2,1)S(1)}, bf16[128,320]{1,0:T(8,128)(2,1)S(1)}, u32[]{:S(2)}, u32[]{:S(2)}) collective-permute-start(bf16[128,320]{1,0:T(8,128)(2,1)S(1)} %get-tuple-element.35.refs_6_), channel_id=1, source_target_pairs={{0,8},{1,9},{2,10},{3,11},{16,24},{17,25},{18,26},{19,27}} | collective-permute-start | bytes 245768 | tf_op jit(solution)/shard_map/ppermute | solution.py:469
  10.9 0.0 collective-permute-done.2.refs_0_.refs_2_
  11.0 0.0 collective-permute-done.3.refs_4_
  11.0 0.0 collective-permute-done.4.refs_5_
  11.0 0.7 %collective-permute-start.5 = (bf16[128,320]{1,0:T(8,128)(2,1)S(1)}, bf16[128,320]{1,0:T(8,128)(2,1)S(1)}, u32[]{:S(2)}, u32[]{:S(2)}) collective-permute-start(bf16[128,320]{1,0:T(8,128)(2,1)S(1)} %get-tuple-element.38.refs_6_), channel_id=1, source_target_pairs={{4,8},{5,9},{6,10},{7,11},{20,24},{21,25},{22,26},{23,27}} | collective-permute-start | bytes 245768 | tf_op jit(solution)/shard_map/ppermute | solution.py:469
  11.7 0.7 %collective-permute-start.7 = (bf16[16,320]{1,0:T(8,128)(2,1)S(1)}, bf16[16,320]{1,0:T(8,128)(2,1)S(1)}, u32[]{:S(2)}, u32[]{:S(2)}) collective-permute-start(bf16[16,320]{1,0:T(8,128)(2,1)S(1)} %get-tuple-element.39), channel_id=1, source_target_pairs={{4,9},{5,10},{6,11},{20,25},{21,26},{22,27}} | collective-permute-start | bytes 30728 | tf_op jit(solution)/shard_map/ppermute | solution.py:469
  12.4 0.7 %collective-permute-start.8 = (bf16[16,320]{1,0:T(8,128)(2,1)S(1)}, bf16[16,320]{1,0:T(8,128)(2,1)S(1)}, u32[]{:S(2)}, u32[]{:S(2)}) collective-permute-start(bf16[16,320]{1,0:T(8,128)(2,1)S(1)} %get-tuple-element.40), channel_id=1, source_target_pairs={{5,8},{6,9},{7,10},{21,24},{22,25},{23,26}} | collective-permute-start | bytes 30728 | tf_op jit(solution)/shard_map/ppermute | solution.py:469
  13.1 1.3 %collective-permute-start.10 = (bf16[128,320]{1,0:T(8,128)(2,1)S(1)}, bf16[128,320]{1,0:T(8,128)(2,1)S(1)}, u32[]{:S(2)}, u32[]{:S(2)}) collective-permute-start(bf16[128,320]{1,0:T(8,128)(2,1)S(1)} %get-tuple-element.38.refs_6_), channel_id=1, source_target_pairs={{4,12},{5,13},{6,14},{7,15},{20,28},{21,29},{22,30},{23,31}} | collective-permute-start | bytes 245768 | tf_op jit(solution)/shard_map/ppermute | solution.py:469
  14.4 0.0 collective-permute-done.6.refs_0_
  14.4 0.0 collective-permute-done.5.refs_1_.refs_2_
  14.4 0.0 collective-permute-done.7.refs_4_
  14.4 0.0 collective-permute-done.8.refs_5_
  14.5 1.3 %collective-permute-start.9 = (bf16[128,320]{1,0:T(8,128)(2,1)S(1)}, bf16[128,320]{1,0:T(8,128)(2,1)S(1)}, u32[]{:S(2)}, u32[]{:S(2)}) collective-permute-start(bf16[128,320]{1,0:T(8,128)(2,1)S(1)} %get-tuple-element.41.refs_6_), channel_id=1, source_target_pairs={{8,12},{9,13},{10,14},{11,15},{24,28},{25,29},{26,30},{27,31}} | collective-permute-start | bytes 245768 | tf_op jit(solution)/shard_map/ppermute | solution.py:469
  15.8 1.3 %collective-permute-start.11 = (bf16[16,320]{1,0:T(8,128)(2,1)S(1)}, bf16[16,320]{1,0:T(8,128)(2,1)S(1)}, u32[]{:S(2)}, u32[]{:S(2)}) collective-permute-start(bf16[16,320]{1,0:T(8,128)(2,1)S(1)} %get-tuple-element.42), channel_id=1, source_target_pairs={{8,13},{9,14},{10,15},{24,29},{25,30},{26,31}} | collective-permute-start | bytes 30728 | tf_op jit(solution)/shard_map/ppermute | solution.py:469
  17.1 1.3 %collective-permute-start.12 = (bf16[16,320]{1,0:T(8,128)(2,1)S(1)}, bf16[16,320]{1,0:T(8,128)(2,1)S(1)}, u32[]{:S(2)}, u32[]{:S(2)}) collective-permute-start(bf16[16,320]{1,0:T(8,128)(2,1)S(1)} %get-tuple-element.43), channel_id=1, source_target_pairs={{9,12},{10,13},{11,14},{25,28},{26,29},{27,30}} | collective-permute-start | bytes 30728 | tf_op jit(solution)/shard_map/ppermute | solution.py:469
  18.4 8.7 %collective-permute-done.10.refs_0_ = bf16[128,320]{1,0:T(8,128)(2,1)S(1)} collective-permute-done((bf16[128,320]{1,0:T(8,128)(2,1)S(1)}, bf16[128,320]{1,0:T(8,128)(2,1)S(1)}, u32[]{:S(2)}, u32[]{:S(2)}) %collective-permute-start.10) | collective-permute-done | bytes 81952 | tf_op jit(solution)/shard_map/ppermute | solution.py:469
  27.0 4.3 %collective-permute-done.9.refs_1_.refs_2_ = bf16[128,320]{1,0:T(8,128)(2,1)S(1)} collective-permute-done((bf16[128,320]{1,0:T(8,128)(2,1)S(1)}, bf16[128,320]{1,0:T(8,128)(2,1)S(1)}, u32[]{:S(2)}, u32[]{:S(2)}) %collective-permute-start.9) | collective-permute-done | bytes 81952 | tf_op jit(solution)/shard_map/ppermute | solution.py:469
  31.3 0.8 %inner.7.refs_3_ = f32[128,320]{1,0:T(8,128)S(1)} custom-call(bf16[128,320]{1,0:T(8,128)(2,1)S(1)} %collective-permute-done.10.refs_0_, bf16[128,320]{1,0:T(8,128)(2,1)S(1)} %collective-permute-done.9.refs_1_.refs_2_, bf16[10,320,320]{2,1,0:T(8,128)(2,1)S(1)} %get-tuple-element.28.refs_1_.refs_7_.refs_2_, f32[8,320]{1,0:T(8,128)S(1)} %bitcast.22, ...), custom_call_target="tpu_custom_call" | custom-call | tf_op jit(solution)/shard_map/inner/pallas_call | solution.py:416
  32.1 0.1 collective-permute-done.11.refs_4_
  32.3 0.9 %collective-permute-done.12.refs_5_ = bf16[16,320]{1,0:T(8,128)(2,1)S(1)} collective-permute-done((bf16[16,320]{1,0:T(8,128)(2,1)S(1)}, bf16[16,320]{1,0:T(8,128)(2,1)S(1)}, u32[]{:S(2)}, u32[]{:S(2)}) %collective-permute-start.12) | collective-permute-done | bytes 10272 | tf_op jit(solution)/shard_map/ppermute | solution.py:469
  33.2 3.0 %outer.7 = (bf16[128,320]{1,0:T(8,128)(2,1)}, bf16[16,320]{1,0:T(8,128)(2,1)}, bf16[16,320]{1,0:T(8,128)(2,1)}) custom-call(s32[2]{0:T(128)S(4)} %get-tuple-element.25.refs_0_, f32[1,5]{1,0:T(1,128)S(4)} %get-tuple-element.26.refs_1_, bf16[128,320]{1,0:T(8,128)(2,1)S(1)} %collective-permute-done.9.refs_1_.refs_2_, f32[128,320]{1,0:T(8,128)S(1)} %inner.7.refs_3_, ...), custom_call_target="tpu_custom_call" | custom-call | tf_op jit(solution)/shard_map/outer/pallas_call | solution.py:435
  (6 shorter events, 0.2 us)
Async XLA Ops:
  0.0 8.2 %collective-permute-start = (bf16[1,128,320]{2,1,0:T(8,128)(2,1)}, bf16[1,128,320]{2,1,0:T(8,128)(2,1)S(1)}, u32[]{:S(2)}, u32[]{:S(2)}) collective-permute-start(bf16[1,128,320]{2,1,0:T(8,128)(2,1)} %bitcast.30), channel_id=1, source_target_pairs={{4,1},{5,2},{6,3},{20,17},{21,18},{22,19}} | collective-permute-start | bytes 245768 | tf_op jit(solution)/shard_map/ppermute | solution.py:469
  0.7 7.5 %collective-permute-start.1 = (bf16[1,128,320]{2,1,0:T(8,128)(2,1)}, bf16[1,128,320]{2,1,0:T(8,128)(2,1)S(1)}, u32[]{:S(2)}, u32[]{:S(2)}) collective-permute-start(bf16[1,128,320]{2,1,0:T(8,128)(2,1)} %bitcast.31), channel_id=1, source_target_pairs={{9,0},{10,1},{11,2},{25,16},{26,17},{27,18}} | collective-permute-start | bytes 245768 | tf_op jit(solution)/shard_map/ppermute | solution.py:469
  8.3 2.7 %collective-permute-start.2 = (bf16[128,320]{1,0:T(8,128)(2,1)S(1)}, bf16[128,320]{1,0:T(8,128)(2,1)S(1)}, u32[]{:S(2)}, u32[]{:S(2)}) collective-permute-start(bf16[128,320]{1,0:T(8,128)(2,1)S(1)} %get-tuple-element.35.refs_6_), channel_id=1, source_target_pairs={{0,4},{1,5},{2,6},{3,7},{16,20},{17,21},{18,22},{19,23}} | collective-permute-start | bytes 245768 | tf_op jit(solution)/shard_map/ppermute | solution.py:469
  8.9 2.1 %collective-permute-start.3 = (bf16[16,320]{1,0:T(8,128)(2,1)S(1)}, bf16[16,320]{1,0:T(8,128)(2,1)S(1)}, u32[]{:S(2)}, u32[]{:S(2)}) collective-permute-start(bf16[16,320]{1,0:T(8,128)(2,1)S(1)} %get-tuple-element.36), channel_id=1, source_target_pairs={{0,5},{1,6},{2,7},{16,21},{17,22},{18,23}} | collective-permute-start | bytes 30728 | tf_op jit(solution)/shard_map/ppermute | solution.py:469
  9.6 1.4 %collective-permute-start.4 = (bf16[16,320]{1,0:T(8,128)(2,1)S(1)}, bf16[16,320]{1,0:T(8,128)(2,1)S(1)}, u32[]{:S(2)}, u32[]{:S(2)}) collective-permute-start(bf16[16,320]{1,0:T(8,128)(2,1)S(1)} %get-tuple-element.37), channel_id=1, source_target_pairs={{1,4},{2,5},{3,6},{17,20},{18,21},{19,22}} | collective-permute-start | bytes 30728 | tf_op jit(solution)/shard_map/ppermute | solution.py:469
  10.3 4.1 %collective-permute-start.6 = (bf16[128,320]{1,0:T(8,128)(2,1)S(1)}, bf16[128,320]{1,0:T(8,128)(2,1)S(1)}, u32[]{:S(2)}, u32[]{:S(2)}) collective-permute-start(bf16[128,320]{1,0:T(8,128)(2,1)S(1)} %get-tuple-element.35.refs_6_), channel_id=1, source_target_pairs={{0,8},{1,9},{2,10},{3,11},{16,24},{17,25},{18,26},{19,27}} | collective-permute-start | bytes 245768 | tf_op jit(solution)/shard_map/ppermute | solution.py:469
  11.0 3.3 %collective-permute-start.5 = (bf16[128,320]{1,0:T(8,128)(2,1)S(1)}, bf16[128,320]{1,0:T(8,128)(2,1)S(1)}, u32[]{:S(2)}, u32[]{:S(2)}) collective-permute-start(bf16[128,320]{1,0:T(8,128)(2,1)S(1)} %get-tuple-element.38.refs_6_), channel_id=1, source_target_pairs={{4,8},{5,9},{6,10},{7,11},{20,24},{21,25},{22,26},{23,27}} | collective-permute-start | bytes 245768 | tf_op jit(solution)/shard_map/ppermute | solution.py:469
  11.7 2.7 %collective-permute-start.7 = (bf16[16,320]{1,0:T(8,128)(2,1)S(1)}, bf16[16,320]{1,0:T(8,128)(2,1)S(1)}, u32[]{:S(2)}, u32[]{:S(2)}) collective-permute-start(bf16[16,320]{1,0:T(8,128)(2,1)S(1)} %get-tuple-element.39), channel_id=1, source_target_pairs={{4,9},{5,10},{6,11},{20,25},{21,26},{22,27}} | collective-permute-start | bytes 30728 | tf_op jit(solution)/shard_map/ppermute | solution.py:469
  12.4 2.0 %collective-permute-start.8 = (bf16[16,320]{1,0:T(8,128)(2,1)S(1)}, bf16[16,320]{1,0:T(8,128)(2,1)S(1)}, u32[]{:S(2)}, u32[]{:S(2)}) collective-permute-start(bf16[16,320]{1,0:T(8,128)(2,1)S(1)} %get-tuple-element.40), channel_id=1, source_target_pairs={{5,8},{6,9},{7,10},{21,24},{22,25},{23,26}} | collective-permute-start | bytes 30728 | tf_op jit(solution)/shard_map/ppermute | solution.py:469
  13.1 14.0 %collective-permute-start.10 = (bf16[128,320]{1,0:T(8,128)(2,1)S(1)}, bf16[128,320]{1,0:T(8,128)(2,1)S(1)}, u32[]{:S(2)}, u32[]{:S(2)}) collective-permute-start(bf16[128,320]{1,0:T(8,128)(2,1)S(1)} %get-tuple-element.38.refs_6_), channel_id=1, source_target_pairs={{4,12},{5,13},{6,14},{7,15},{20,28},{21,29},{22,30},{23,31}} | collective-permute-start | bytes 245768 | tf_op jit(solution)/shard_map/ppermute | solution.py:469
  14.5 16.8 %collective-permute-start.9 = (bf16[128,320]{1,0:T(8,128)(2,1)S(1)}, bf16[128,320]{1,0:T(8,128)(2,1)S(1)}, u32[]{:S(2)}, u32[]{:S(2)}) collective-permute-start(bf16[128,320]{1,0:T(8,128)(2,1)S(1)} %get-tuple-element.41.refs_6_), channel_id=1, source_target_pairs={{8,12},{9,13},{10,14},{11,15},{24,28},{25,29},{26,30},{27,31}} | collective-permute-start | bytes 245768 | tf_op jit(solution)/shard_map/ppermute | solution.py:469
  15.8 16.5 %collective-permute-start.11 = (bf16[16,320]{1,0:T(8,128)(2,1)S(1)}, bf16[16,320]{1,0:T(8,128)(2,1)S(1)}, u32[]{:S(2)}, u32[]{:S(2)}) collective-permute-start(bf16[16,320]{1,0:T(8,128)(2,1)S(1)} %get-tuple-element.42), channel_id=1, source_target_pairs={{8,13},{9,14},{10,15},{24,29},{25,30},{26,31}} | collective-permute-start | bytes 30728 | tf_op jit(solution)/shard_map/ppermute | solution.py:469
  17.1 16.1 %collective-permute-start.12 = (bf16[16,320]{1,0:T(8,128)(2,1)S(1)}, bf16[16,320]{1,0:T(8,128)(2,1)S(1)}, u32[]{:S(2)}, u32[]{:S(2)}) collective-permute-start(bf16[16,320]{1,0:T(8,128)(2,1)S(1)} %get-tuple-element.43), channel_id=1, source_target_pairs={{9,12},{10,13},{11,14},{25,28},{26,29},{27,30}} | collective-permute-start | bytes 30728 | tf_op jit(solution)/shard_map/ppermute | solution.py:469

commit v3 on v1

--- a/solution.py
+++ b/solution.py
@@ -74,8 +74,8 @@
         pltpu.make_async_copy(source, target, sems.at[place])
         for place, (source, target) in enumerate(zip(sources, targets))
     ]
-    for copy in copies:
-        copy.start()
+    for place in (1, 0, *range(2, len(copies))):
+        copies[place].start()
     part = conv_ref.shape[-1]
 
     def rule(i, a, b):

time: 36.6 us -> 34.7 us (0.948)
  waiting for transfers between devices: 14 us -> 12.1 us
    ppermute x13, waiting for transfers between devices: 14 us -> 12.1 us  [pass_on(): return lax.ppermute(value, axes, links)]
  transfers between devices with their start and end apart: 13 -> 13, of which waited for: 4 -> 3; matrix products, arithmetic and copies ran while one was open for 0% -> 0% of each run, Pallas kernels for 16% -> 17%
where the time goes in v3:
time: 34.7 us; the launch traced here: 34.4 us
  waiting for transfers between devices  12.1 us (35%)
  starting transfers between devices  11.1 us (32%)
  Pallas kernels  8.95 us (26%)
  between operations  2.18 us (6%)
    ppermute x13, waiting for transfers between devices, pass_on(): return lax.ppermute(value, axes, links)  12.1 us
    ppermute x13, starting transfers between devices, pass_on(): return lax.ppermute(value, axes, links)  11.1 us
    pallas_call x1, Pallas kernels, section_weights(): pl.pallas_call(functools.partial(weights_kernel, first_skip), out_shape=(...  5.02 us
    pallas_call x4, Pallas kernels, run_outer(): pl.pallas_call(functools.partial(outer_kernel, columns, tick if static el...  3.05 us
    pallas_call x4, Pallas kernels, run_inner(): pl.pallas_call(functools.partial(inner_kernel, columns, tick if static el...  0.88 us
  transfers between devices with their start and end apart: 13, of which 3 were waited for; matrix products, arithmetic and copies ran while one was open for 0% of the time, Pallas kernels for 17%

profile of v3, /device:TPU:29, one launch (start us, length us, event | category | flops | bytes accessed | tf_op | source)
XLA Modules:
  0.0 34.4 jit_solution(14804098552256153353)
XLA Ops:
  0.0 0.7 %collective-permute-start = (bf16[1,128,320]{2,1,0:T(8,128)(2,1)}, bf16[1,128,320]{2,1,0:T(8,128)(2,1)S(1)}, u32[]{:S(2)}, u32[]{:S(2)}) collective-permute-start(bf16[1,128,320]{2,1,0:T(8,128)(2,1)} %bitcast.30), channel_id=1, source_target_pairs={{4,1},{5,2},{6,3},{20,17},{21,18},{22,19}} | collective-permute-start | bytes 245768 | tf_op jit(solution)/shard_map/ppermute | solution.py:469
  0.7 0.7 %collective-permute-start.1 = (bf16[1,128,320]{2,1,0:T(8,128)(2,1)}, bf16[1,128,320]{2,1,0:T(8,128)(2,1)S(1)}, u32[]{:S(2)}, u32[]{:S(2)}) collective-permute-start(bf16[1,128,320]{2,1,0:T(8,128)(2,1)} %bitcast.31), channel_id=1, source_target_pairs={{9,0},{10,1},{11,2},{25,16},{26,17},{27,18}} | collective-permute-start | bytes 245768 | tf_op jit(solution)/shard_map/ppermute | solution.py:469
  3.3 5.0 %weights.1 = (bf16[10,320,320]{2,1,0:T(8,128)(2,1)S(1)}, bf16[320,1024]{1,0:T(8,128)(2,1)S(1)}, bf16[320,320]{1,0:T(8,128)(2,1)S(1)}, bf16[320,1280]{1,0:T(8,128...) custom-call(f32[4,4,4]{2,1,0:T(4,128)} %bitcast.34, ...), custom_call_target="tpu_custom_call" | custom-call | tf_op jit(solution)/shard_map/weights/pallas_call | solution.py:233
  8.3 0.0 collective-permute-done
  8.3 0.0 collective-permute-done.1
  8.4 0.7 %collective-permute-start.2 = (bf16[128,320]{1,0:T(8,128)(2,1)S(1)}, bf16[128,320]{1,0:T(8,128)(2,1)S(1)}, u32[]{:S(2)}, u32[]{:S(2)}) collective-permute-start(bf16[128,320]{1,0:T(8,128)(2,1)S(1)} %get-tuple-element.35.refs_6_), channel_id=1, source_target_pairs={{0,4},{1,5},{2,6},{3,7},{16,20},{17,21},{18,22},{19,23}} | collective-permute-start | bytes 245768 | tf_op jit(solution)/shard_map/ppermute | solution.py:469
  9.1 0.7 %collective-permute-start.3 = (bf16[16,320]{1,0:T(8,128)(2,1)S(1)}, bf16[16,320]{1,0:T(8,128)(2,1)S(1)}, u32[]{:S(2)}, u32[]{:S(2)}) collective-permute-start(bf16[16,320]{1,0:T(8,128)(2,1)S(1)} %get-tuple-element.36), channel_id=1, source_target_pairs={{0,5},{1,6},{2,7},{16,21},{17,22},{18,23}} | collective-permute-start | bytes 30728 | tf_op jit(solution)/shard_map/ppermute | solution.py:469
  9.7 0.7 %collective-permute-start.4 = (bf16[16,320]{1,0:T(8,128)(2,1)S(1)}, bf16[16,320]{1,0:T(8,128)(2,1)S(1)}, u32[]{:S(2)}, u32[]{:S(2)}) collective-permute-start(bf16[16,320]{1,0:T(8,128)(2,1)S(1)} %get-tuple-element.37), channel_id=1, source_target_pairs={{1,4},{2,5},{3,6},{17,20},{18,21},{19,22}} | collective-permute-start | bytes 30728 | tf_op jit(solution)/shard_map/ppermute | solution.py:469
  10.4 0.7 %collective-permute-start.6 = (bf16[128,320]{1,0:T(8,128)(2,1)S(1)}, bf16[128,320]{1,0:T(8,128)(2,1)S(1)}, u32[]{:S(2)}, u32[]{:S(2)}) collective-permute-start(bf16[128,320]{1,0:T(8,128)(2,1)S(1)} %get-tuple-element.35.refs_6_), channel_id=1, source_target_pairs={{0,8},{1,9},{2,10},{3,11},{16,24},{17,25},{18,26},{19,27}} | collective-permute-start | bytes 245768 | tf_op jit(solution)/shard_map/ppermute | solution.py:469
  11.1 0.0 collective-permute-done.2.refs_0_.refs_2_
  11.1 0.0 collective-permute-done.3.refs_4_
  11.1 0.0 collective-permute-done.4.refs_5_
  11.2 0.7 %collective-permute-start.5 = (bf16[128,320]{1,0:T(8,128)(2,1)S(1)}, bf16[128,320]{1,0:T(8,128)(2,1)S(1)}, u32[]{:S(2)}, u32[]{:S(2)}) collective-permute-start(bf16[128,320]{1,0:T(8,128)(2,1)S(1)} %get-tuple-element.38.refs_6_), channel_id=1, source_target_pairs={{4,8},{5,9},{6,10},{7,11},{20,24},{21,25},{22,26},{23,27}} | collective-permute-start | bytes 245768 | tf_op jit(solution)/shard_map/ppermute | solution.py:469
  11.8 0.7 %collective-permute-start.7 = (bf16[16,320]{1,0:T(8,128)(2,1)S(1)}, bf16[16,320]{1,0:T(8,128)(2,1)S(1)}, u32[]{:S(2)}, u32[]{:S(2)}) collective-permute-start(bf16[16,320]{1,0:T(8,128)(2,1)S(1)} %get-tuple-element.39), channel_id=1, source_target_pairs={{4,9},{5,10},{6,11},{20,25},{21,26},{22,27}} | collective-permute-start | bytes 30728 | tf_op jit(solution)/shard_map/ppermute | solution.py:469
  12.5 0.7 %collective-permute-start.8 = (bf16[16,320]{1,0:T(8,128)(2,1)S(1)}, bf16[16,320]{1,0:T(8,128)(2,1)S(1)}, u32[]{:S(2)}, u32[]{:S(2)}) collective-permute-start(bf16[16,320]{1,0:T(8,128)(2,1)S(1)} %get-tuple-element.40), channel_id=1, source_target_pairs={{5,8},{6,9},{7,10},{21,24},{22,25},{23,26}} | collective-permute-start | bytes 30728 | tf_op jit(solution)/shard_map/ppermute | solution.py:469
  13.2 1.3 %collective-permute-start.10 = (bf16[128,320]{1,0:T(8,128)(2,1)S(1)}, bf16[128,320]{1,0:T(8,128)(2,1)S(1)}, u32[]{:S(2)}, u32[]{:S(2)}) collective-permute-start(bf16[128,320]{1,0:T(8,128)(2,1)S(1)} %get-tuple-element.38.refs_6_), channel_id=1, source_target_pairs={{4,12},{5,13},{6,14},{7,15},{20,28},{21,29},{22,30},{23,31}} | collective-permute-start | bytes 245768 | tf_op jit(solution)/shard_map/ppermute | solution.py:469
  14.5 0.0 collective-permute-done.6.refs_0_
  14.5 0.0 collective-permute-done.5.refs_1_.refs_2_
  14.5 0.0 collective-permute-done.7.refs_4_
  14.5 0.0 collective-permute-done.8.refs_5_
  14.6 1.3 %collective-permute-start.9 = (bf16[128,320]{1,0:T(8,128)(2,1)S(1)}, bf16[128,320]{1,0:T(8,128)(2,1)S(1)}, u32[]{:S(2)}, u32[]{:S(2)}) collective-permute-start(bf16[128,320]{1,0:T(8,128)(2,1)S(1)} %get-tuple-element.41.refs_6_), channel_id=1, source_target_pairs={{8,12},{9,13},{10,14},{11,15},{24,28},{25,29},{26,30},{27,31}} | collective-permute-start | bytes 245768 | tf_op jit(solution)/shard_map/ppermute | solution.py:469
  15.9 1.3 %collective-permute-start.11 = (bf16[16,320]{1,0:T(8,128)(2,1)S(1)}, bf16[16,320]{1,0:T(8,128)(2,1)S(1)}, u32[]{:S(2)}, u32[]{:S(2)}) collective-permute-start(bf16[16,320]{1,0:T(8,128)(2,1)S(1)} %get-tuple-element.42), channel_id=1, source_target_pairs={{8,13},{9,14},{10,15},{24,29},{25,30},{26,31}} | collective-permute-start | bytes 30728 | tf_op jit(solution)/shard_map/ppermute | solution.py:469
  17.2 1.3 %collective-permute-start.12 = (bf16[16,320]{1,0:T(8,128)(2,1)S(1)}, bf16[16,320]{1,0:T(8,128)(2,1)S(1)}, u32[]{:S(2)}, u32[]{:S(2)}) collective-permute-start(bf16[16,320]{1,0:T(8,128)(2,1)S(1)} %get-tuple-element.43), channel_id=1, source_target_pairs={{9,12},{10,13},{11,14},{25,28},{26,29},{27,30}} | collective-permute-start | bytes 30728 | tf_op jit(solution)/shard_map/ppermute | solution.py:469
  18.5 8.6 %collective-permute-done.10.refs_0_ = bf16[128,320]{1,0:T(8,128)(2,1)S(1)} collective-permute-done((bf16[128,320]{1,0:T(8,128)(2,1)S(1)}, bf16[128,320]{1,0:T(8,128)(2,1)S(1)}, u32[]{:S(2)}, u32[]{:S(2)}) %collective-permute-start.10) | collective-permute-done | bytes 81952 | tf_op jit(solution)/shard_map/ppermute | solution.py:469
  27.1 2.6 %collective-permute-done.9.refs_1_.refs_2_ = bf16[128,320]{1,0:T(8,128)(2,1)S(1)} collective-permute-done((bf16[128,320]{1,0:T(8,128)(2,1)S(1)}, bf16[128,320]{1,0:T(8,128)(2,1)S(1)}, u32[]{:S(2)}, u32[]{:S(2)}) %collective-permute-start.9) | collective-permute-done | bytes 81952 | tf_op jit(solution)/shard_map/ppermute | solution.py:469
  29.7 0.8 %inner.7.refs_3_ = f32[128,320]{1,0:T(8,128)S(1)} custom-call(bf16[128,320]{1,0:T(8,128)(2,1)S(1)} %collective-permute-done.10.refs_0_, bf16[128,320]{1,0:T(8,128)(2,1)S(1)} %collective-permute-done.9.refs_1_.refs_2_, bf16[10,320,320]{2,1,0:T(8,128)(2,1)S(1)} %get-tuple-element.28.refs_1_.refs_7_.refs_2_, f32[8,320]{1,0:T(8,128)S(1)} %bitcast.22, ...), custom_call_target="tpu_custom_call" | custom-call | tf_op jit(solution)/shard_map/inner/pallas_call | solution.py:416
  30.5 0.0 collective-permute-done.11.refs_4_
  30.5 0.9 %collective-permute-done.12.refs_5_ = bf16[16,320]{1,0:T(8,128)(2,1)S(1)} collective-permute-done((bf16[16,320]{1,0:T(8,128)(2,1)S(1)}, bf16[16,320]{1,0:T(8,128)(2,1)S(1)}, u32[]{:S(2)}, u32[]{:S(2)}) %collective-permute-start.12) | collective-permute-done | bytes 10272 | tf_op jit(solution)/shard_map/ppermute | solution.py:469
  31.5 3.0 %outer.7 = (bf16[128,320]{1,0:T(8,128)(2,1)}, bf16[16,320]{1,0:T(8,128)(2,1)}, bf16[16,320]{1,0:T(8,128)(2,1)}) custom-call(s32[2]{0:T(128)S(4)} %get-tuple-element.25.refs_0_, f32[1,5]{1,0:T(1,128)S(4)} %get-tuple-element.26.refs_1_, bf16[128,320]{1,0:T(8,128)(2,1)S(1)} %collective-permute-done.9.refs_1_.refs_2_, f32[128,320]{1,0:T(8,128)S(1)} %inner.7.refs_3_, ...), custom_call_target="tpu_custom_call" | custom-call | tf_op jit(solution)/shard_map/outer/pallas_call | solution.py:435
  (6 shorter events, 0.2 us)
Async XLA Ops:
  0.0 8.3 %collective-permute-start = (bf16[1,128,320]{2,1,0:T(8,128)(2,1)}, bf16[1,128,320]{2,1,0:T(8,128)(2,1)S(1)}, u32[]{:S(2)}, u32[]{:S(2)}) collective-permute-start(bf16[1,128,320]{2,1,0:T(8,128)(2,1)} %bitcast.30), channel_id=1, source_target_pairs={{4,1},{5,2},{6,3},{20,17},{21,18},{22,19}} | collective-permute-start | bytes 245768 | tf_op jit(solution)/shard_map/ppermute | solution.py:469
  0.7 7.7 %collective-permute-start.1 = (bf16[1,128,320]{2,1,0:T(8,128)(2,1)}, bf16[1,128,320]{2,1,0:T(8,128)(2,1)S(1)}, u32[]{:S(2)}, u32[]{:S(2)}) collective-permute-start(bf16[1,128,320]{2,1,0:T(8,128)(2,1)} %bitcast.31), channel_id=1, source_target_pairs={{9,0},{10,1},{11,2},{25,16},{26,17},{27,18}} | collective-permute-start | bytes 245768 | tf_op jit(solution)/shard_map/ppermute | solution.py:469
  8.4 2.7 %collective-permute-start.2 = (bf16[128,320]{1,0:T(8,128)(2,1)S(1)}, bf16[128,320]{1,0:T(8,128)(2,1)S(1)}, u32[]{:S(2)}, u32[]{:S(2)}) collective-permute-start(bf16[128,320]{1,0:T(8,128)(2,1)S(1)} %get-tuple-element.35.refs_6_), channel_id=1, source_target_pairs={{0,4},{1,5},{2,6},{3,7},{16,20},{17,21},{18,22},{19,23}} | collective-permute-start | bytes 245768 | tf_op jit(solution)/shard_map/ppermute | solution.py:469
  9.1 2.1 %collective-permute-start.3 = (bf16[16,320]{1,0:T(8,128)(2,1)S(1)}, bf16[16,320]{1,0:T(8,128)(2,1)S(1)}, u32[]{:S(2)}, u32[]{:S(2)}) collective-permute-start(bf16[16,320]{1,0:T(8,128)(2,1)S(1)} %get-tuple-element.36), channel_id=1, source_target_pairs={{0,5},{1,6},{2,7},{16,21},{17,22},{18,23}} | collective-permute-start | bytes 30728 | tf_op jit(solution)/shard_map/ppermute | solution.py:469
  9.7 1.4 %collective-permute-start.4 = (bf16[16,320]{1,0:T(8,128)(2,1)S(1)}, bf16[16,320]{1,0:T(8,128)(2,1)S(1)}, u32[]{:S(2)}, u32[]{:S(2)}) collective-permute-start(bf16[16,320]{1,0:T(8,128)(2,1)S(1)} %get-tuple-element.37), channel_id=1, source_target_pairs={{1,4},{2,5},{3,6},{17,20},{18,21},{19,22}} | collective-permute-start | bytes 30728 | tf_op jit(solution)/shard_map/ppermute | solution.py:469
  10.4 4.1 %collective-permute-start.6 = (bf16[128,320]{1,0:T(8,128)(2,1)S(1)}, bf16[128,320]{1,0:T(8,128)(2,1)S(1)}, u32[]{:S(2)}, u32[]{:S(2)}) collective-permute-start(bf16[128,320]{1,0:T(8,128)(2,1)S(1)} %get-tuple-element.35.refs_6_), channel_id=1, source_target_pairs={{0,8},{1,9},{2,10},{3,11},{16,24},{17,25},{18,26},{19,27}} | collective-permute-start | bytes 245768 | tf_op jit(solution)/shard_map/ppermute | solution.py:469
  11.2 3.3 %collective-permute-start.5 = (bf16[128,320]{1,0:T(8,128)(2,1)S(1)}, bf16[128,320]{1,0:T(8,128)(2,1)S(1)}, u32[]{:S(2)}, u32[]{:S(2)}) collective-permute-start(bf16[128,320]{1,0:T(8,128)(2,1)S(1)} %get-tuple-element.38.refs_6_), channel_id=1, source_target_pairs={{4,8},{5,9},{6,10},{7,11},{20,24},{21,25},{22,26},{23,27}} | collective-permute-start | bytes 245768 | tf_op jit(solution)/shard_map/ppermute | solution.py:469
  11.8 2.7 %collective-permute-start.7 = (bf16[16,320]{1,0:T(8,128)(2,1)S(1)}, bf16[16,320]{1,0:T(8,128)(2,1)S(1)}, u32[]{:S(2)}, u32[]{:S(2)}) collective-permute-start(bf16[16,320]{1,0:T(8,128)(2,1)S(1)} %get-tuple-element.39), channel_id=1, source_target_pairs={{4,9},{5,10},{6,11},{20,25},{21,26},{22,27}} | collective-permute-start | bytes 30728 | tf_op jit(solution)/shard_map/ppermute | solution.py:469
  12.5 2.0 %collective-permute-start.8 = (bf16[16,320]{1,0:T(8,128)(2,1)S(1)}, bf16[16,320]{1,0:T(8,128)(2,1)S(1)}, u32[]{:S(2)}, u32[]{:S(2)}) collective-permute-start(bf16[16,320]{1,0:T(8,128)(2,1)S(1)} %get-tuple-element.40), channel_id=1, source_target_pairs={{5,8},{6,9},{7,10},{21,24},{22,25},{23,26}} | collective-permute-start | bytes 30728 | tf_op jit(solution)/shard_map/ppermute | solution.py:469
  13.2 13.9 %collective-permute-start.10 = (bf16[128,320]{1,0:T(8,128)(2,1)S(1)}, bf16[128,320]{1,0:T(8,128)(2,1)S(1)}, u32[]{:S(2)}, u32[]{:S(2)}) collective-permute-start(bf16[128,320]{1,0:T(8,128)(2,1)S(1)} %get-tuple-element.38.refs_6_), channel_id=1, source_target_pairs={{4,12},{5,13},{6,14},{7,15},{20,28},{21,29},{22,30},{23,31}} | collective-permute-start | bytes 245768 | tf_op jit(solution)/shard_map/ppermute | solution.py:469
  14.6 15.1 %collective-permute-start.9 = (bf16[128,320]{1,0:T(8,128)(2,1)S(1)}, bf16[128,320]{1,0:T(8,128)(2,1)S(1)}, u32[]{:S(2)}, u32[]{:S(2)}) collective-permute-start(bf16[128,320]{1,0:T(8,128)(2,1)S(1)} %get-tuple-element.41.refs_6_), channel_id=1, source_target_pairs={{8,12},{9,13},{10,14},{11,15},{24,28},{25,29},{26,30},{27,31}} | collective-permute-start | bytes 245768 | tf_op jit(solution)/shard_map/ppermute | solution.py:469
  15.9 14.6 %collective-permute-start.11 = (bf16[16,320]{1,0:T(8,128)(2,1)S(1)}, bf16[16,320]{1,0:T(8,128)(2,1)S(1)}, u32[]{:S(2)}, u32[]{:S(2)}) collective-permute-start(bf16[16,320]{1,0:T(8,128)(2,1)S(1)} %get-tuple-element.42), channel_id=1, source_target_pairs={{8,13},{9,14},{10,15},{24,29},{25,30},{26,31}} | collective-permute-start | bytes 30728 | tf_op jit(solution)/shard_map/ppermute | solution.py:469
  17.2 14.3 %collective-permute-start.12 = (bf16[16,320]{1,0:T(8,128)(2,1)S(1)}, bf16[16,320]{1,0:T(8,128)(2,1)S(1)}, u32[]{:S(2)}, u32[]{:S(2)}) collective-permute-start(bf16[16,320]{1,0:T(8,128)(2,1)S(1)} %get-tuple-element.43), channel_id=1, source_target_pairs={{9,12},{10,13},{11,14},{25,28},{26,29},{27,30}} | collective-permute-start | bytes 30728 | tf_op jit(solution)/shard_map/ppermute | solution.py:469
